TPU v7x, 512 devices: a whole 4x4x16 slice. The times are simulated.
512 devices in a mesh: seq: 64 (over z_lo, y, core), tensor: 8 (over z_hi, x).
Axes of the slice: x: 4, y: 4, z: 16 (z_hi: 2, z_lo: 8; z = z_hi * 8 + z_lo), core: 2. Of those that a mesh axis runs over, the one named last changes fastest.
Arguments:
- queries: bfloat16 [16384, 4096], P('seq', 'tensor'), may hold values from -9 to 9
- key_rows: bfloat16 [16384, 1024], P('seq', 'tensor'), may hold values from -9 to 9
- value_rows: bfloat16 [16384, 1024], P('seq', 'tensor'), may hold values from -6 to 6
- out_weight: bfloat16 [4096, 4096], P(('tensor', 'seq')), may hold values from -0.09375 to 0.09375
- out_grad: bfloat16 [16384, 4096], P('seq', 'tensor'), may hold values from -6 to 6
- doc_lengths: int32 [128], replicated, may hold values from 1 to 1024, 16384 in all
Outputs:
- attn_out: bfloat16 [16384, 4096], P('seq', 'tensor')
- grad_queries: bfloat16 [16384, 4096], P('seq', 'tensor')
- grad_keys: bfloat16 [16384, 1024], P('seq', 'tensor')
- grad_values: bfloat16 [16384, 1024], P('seq', 'tensor')
Inputs may be any that keep to these rules, and one draw needn't show every extreme that they name: `doc_lengths`: the lengths sum to 16384; the longest is exactly 1024.
All inputs are finite; a program needn't handle non-finite values.
Results may differ from a plain program's by a relative error of at most 0.025.
Values may be sent and summed in bfloat16 or wider, within the bound.
A program may use at most 64 MiB of HBM per device.

v0:
```python
import math

import jax
import jax.numpy as jnp
from jax import lax
from jax.sharding import PartitionSpec as P

DH = 128
SPAN = 4


NEG_FILL = -1e30


def shifted(value, axis, steps):
    count = lax.axis_size(axis)
    leading, last = (max(0, -steps), min(count, count - steps))
    return lax.ppermute(value, axis, [(source, source + steps) for source in range(leading, last)])


def doc_index(positions, doc_lengths):
    doc_ends = jnp.cumsum(doc_lengths)
    counted = jnp.sum((doc_ends[None, :] <= positions[:, None]).astype(jnp.int32), axis=1)
    return jnp.where(positions < 0, -1, counted)


def local(queries, key_rows, value_rows, out_weight, out_grad, doc_lengths):
    row_count = queries.shape[0]
    kv_width = key_rows.shape[1]
    kv_heads = kv_width // DH
    q_heads = queries.shape[1] // DH
    group_size = q_heads // kv_heads
    score_scale = 1.0 / math.sqrt(DH)
    seq_index = lax.axis_index("seq")
    local_place = seq_index * row_count + jnp.arange(row_count, dtype=jnp.int32)
    query_docs = doc_index(local_place, doc_lengths)
    query_heads = queries.reshape(row_count, kv_heads, group_size, DH)
    local_pair = jnp.stack([key_rows, value_rows])
    pair_list = [local_pair]
    moving = local_pair
    for distance in range(1, SPAN + 1):
        moving = shifted(moving, "seq", 1)
        pair_list.append(moving)
    visibility = []
    for distance in range(SPAN + 1):
        key_place = local_place - distance * row_count
        key_docs = doc_index(key_place, doc_lengths)
        visibility.append(
            (query_docs[:, None] == key_docs[None, :])
            & (key_place[None, :] <= local_place[:, None])
        )

    def block_scores(kv_pair, visible):
        keys_here = kv_pair[0].reshape(row_count, kv_heads, DH)
        scores = (
            jnp.einsum("rkgd,wkd->kgrw", query_heads, keys_here, preferred_element_type=jnp.float32)
            * score_scale
        )
        return jnp.where(visible[None, None], scores, NEG_FILL)

    def block_stats(kv_pair, visible):
        scores = block_scores(kv_pair, visible)
        block_top = jnp.max(scores, axis=3)
        block_total = jnp.sum(
            jnp.where(visible[None, None], jnp.exp(scores - block_top[..., None]), 0.0), axis=3
        )
        return (block_top, block_total)

    stat_shape = (kv_heads, group_size, row_count)
    stat_empty = (jnp.full(stat_shape, NEG_FILL, jnp.float32), jnp.zeros(stat_shape, jnp.float32))
    running_top, running_total = stat_empty
    for kv_pair, visible in zip(pair_list, visibility):
        block_top, block_total = block_stats(kv_pair, visible)
        new_top = jnp.maximum(running_top, block_top)
        running_total = running_total * jnp.exp(running_top - new_top) + block_total * jnp.exp(
            block_top - new_top
        )
        running_top = new_top
    log_total = running_top + jnp.log(running_total)
    head_shape = (row_count, kv_heads, group_size, DH)

    def block_context(kv_pair, visible):
        scores = block_scores(kv_pair, visible)
        weights = jnp.where(
            visible[None, None], jnp.exp(scores - log_total[..., None]), 0.0
        ).astype(jnp.bfloat16)
        values_here = kv_pair[1].reshape(row_count, kv_heads, DH)
        return jnp.einsum(
            "kgrw,wkd->rkgd", weights, values_here, preferred_element_type=jnp.float32
        )

    context_sum = jnp.zeros(head_shape, jnp.float32)
    for kv_pair, visible in zip(pair_list, visibility):
        context_sum = context_sum + block_context(kv_pair, visible)
    context_heads = context_sum.astype(jnp.bfloat16)
    context = context_heads.reshape(row_count, q_heads * DH)
    partial_value = jnp.dot(
        context,
        lax.all_gather(out_weight, "seq", axis=0, tiled=True),
        preferred_element_type=jnp.float32,
    )
    rounded = lax.optimization_barrier(partial_value.astype(jnp.bfloat16)).astype(jnp.float32)
    attn_out = lax.psum_scatter(
        rounded.astype(jnp.bfloat16), "tensor", scatter_dimension=1, tiled=True
    )
    grad_rows = lax.all_gather(out_grad, "tensor", axis=1, tiled=True)
    contract_last = (((1,), (1,)), ((), ()))
    grad_context = lax.dot_general(
        grad_rows,
        lax.all_gather(out_weight, "seq", axis=0, tiled=True),
        contract_last,
        preferred_element_type=jnp.float32,
    )
    grad_heads = grad_context.astype(jnp.bfloat16).reshape(head_shape)
    row_delta = jnp.transpose(
        jnp.sum(grad_heads.astype(jnp.float32) * context_heads.astype(jnp.float32), axis=3),
        (1, 2, 0),
    )

    def block_grads(kv_pair, visible):
        keys_here = kv_pair[0].reshape(row_count, kv_heads, DH)
        values_here = kv_pair[1].reshape(row_count, kv_heads, DH)
        scores = block_scores(kv_pair, visible)
        probabilities = jnp.where(visible[None, None], jnp.exp(scores - log_total[..., None]), 0.0)
        weights = probabilities.astype(jnp.bfloat16)
        prob_grad = jnp.einsum(
            "rkgd,wkd->kgrw", grad_heads, values_here, preferred_element_type=jnp.float32
        )
        score_grad = (probabilities * (prob_grad - row_delta[..., None])).astype(jnp.bfloat16)
        query_part = jnp.einsum(
            "kgrw,wkd->rkgd", score_grad, keys_here, preferred_element_type=jnp.float32
        )
        key_part = jnp.einsum(
            "kgrw,rkgd->wkd", score_grad, query_heads, preferred_element_type=jnp.float32
        )
        value_part = jnp.einsum(
            "kgrw,rkgd->wkd", weights, grad_heads, preferred_element_type=jnp.float32
        )
        return (
            query_part,
            jnp.stack(
                [key_part.reshape(row_count, kv_width), value_part.reshape(row_count, kv_width)]
            ),
        )

    query_sum = jnp.zeros(head_shape, jnp.float32)
    pair_grads = []
    for kv_pair, visible in zip(pair_list, visibility):
        query_part, pair_part = block_grads(kv_pair, visible)
        query_sum = query_sum + query_part
        pair_grads.append(pair_part)
    carried = pair_grads[SPAN]
    for distance in range(SPAN - 1, -1, -1):
        carried = (
            shifted(carried.astype(jnp.bfloat16), "seq", -1).astype(carried.dtype)
            + pair_grads[distance]
        )
    grad_queries = (query_sum * score_scale).astype(jnp.bfloat16).reshape(row_count, q_heads * DH)
    grad_keys = (carried[0] * score_scale).astype(jnp.bfloat16)
    grad_values = carried[1].astype(jnp.bfloat16)
    return (attn_out, grad_queries, grad_keys, grad_values)


def solution(mesh):
    placed = (
        P("seq", "tensor"),
        P("seq", "tensor"),
        P("seq", "tensor"),
        P(("tensor", "seq"), None),
        P("seq", "tensor"),
        P(),
    )
    return jax.shard_map(
        local,
        mesh=mesh,
        in_specs=placed,
        out_specs=(P("seq", "tensor"), P("seq", "tensor"), P("seq", "tensor"), P("seq", "tensor")),
        check_vma=False,
    )
```

profile of v0, /device:TPU:9, one launch (start us, length us, event | category | flops | bytes accessed | tf_op | source)
XLA Modules:
  0.0 416.0 jit_solution(17635484042564774873)
XLA Ops:
  7.2 0.7 all-gather.5.cloned.1.call-update
  8.0 0.7 all-gather.3.cloned.1.call-update
  8.7 0.9 pad_maximum_fusion
  9.6 3.8 collective-permute-start
  13.4 0.8 copy.118
  14.5 0.5 convert_reduce_fusion.3
  15.0 0.5 compare_and_fusion.3
  15.6 1.2 fusion.124
  17.0 2.6 collective-permute-start.1
  19.6 0.3 fusion.127
  20.0 0.2 select_reduce_fusion.3
  20.2 1.4 collective-permute-done.1
  21.6 4.3 %collective-permute-start.2 = (bf16[2,256,128]{2,1,0:T(8,128)(2,1)S(1)}, bf16[2,256,128]{2,1,0:T(8,128)(2,1)S(1)}, u32[]{:S(2)}, u32[]{:S(2)}) collective-permute-start(bf16[2,256,128]{2,1,0:T(8,128)(2,1)S(1)} %collective-permute-done.1), channel_id=1, source_target_pairs={{0,8},{8,16},{16,24},{24,32},{32,40},{40,48},{48,56},{56,64},{64,7... | collective-permute-start | bytes 393224 | tf_op jit(solution)/shard_map/ppermute | solution.py:18
  25.9 0.3 fusion.126
  26.3 0.2 select_reduce_fusion.2
  26.5 1.4 collective-permute-done.2
  27.9 4.3 %collective-permute-start.3 = (bf16[2,256,128]{2,1,0:T(8,128)(2,1)S(1)}, bf16[2,256,128]{2,1,0:T(8,128)(2,1)S(1)}, u32[]{:S(2)}, u32[]{:S(2)}) collective-permute-start(bf16[2,256,128]{2,1,0:T(8,128)(2,1)S(1)} %collective-permute-done.2), channel_id=1, source_target_pairs={{0,8},{8,16},{16,24},{24,32},{32,40},{40,48},{48,56},{56,64},{64,7... | collective-permute-start | bytes 393224 | tf_op jit(solution)/shard_map/ppermute | solution.py:18
  32.2 0.3 fusion.125
  32.7 1.4 collective-permute-done.3
  34.1 0.3 fusion.123
  34.5 1.0 copy-done.1
  35.7 0.3 convolution_bitcast_fusion.6
  36.1 0.3 convolution_add_fusion.7
  36.4 0.3 convolution_add_fusion.6
  36.8 1.2 convolution_add_fusion.5
  38.0 90.4 %all-gather.5.cloned.1.call-done = bf16[256,4096]{1,0:T(8,128)(2,1)} async-done(((bf16[256,512]{1,0:T(8,128)(2,1)}), bf16[256,4096]{1,0:T(8,128)(2,1)}) %all-gather.5.cloned.1.call-update) | async-done | bytes 2097168 | tf_op jit(solution)/shard_map/all_gather | solution.py:106
  128.3 124.0 %all-gather.3.cloned.1.call-done = bf16[512,4096]{1,0:T(8,128)(2,1)} async-done(((bf16[8,4096]{1,0:T(8,128)(2,1)}), bf16[512,4096]{1,0:T(8,128)(2,1)}) %all-gather.3.cloned.1.call-update) | async-done | bytes 4194320 | tf_op jit(solution)/shard_map/all_gather | solution.py:99
  252.3 4.8 %convolution_convert_fusion.1 = bf16[256,512]{1,0:T(8,128)(2,1)} fusion(bf16[256,4096]{1,0:T(8,128)(2,1)} %all-gather.5.cloned.1.call-done, bf16[512,4096]{1,0:T(8,128)(2,1)} %all-gather.3.cloned.1.call-done), kind=kOutput, calls=%fused_computation.53 | convolution fusion | flops 1073872896 | bytes 6553600 | tf_op jit(solution)/shard_map/dot_general | solution.py:108
  257.1 1.8 copy.218
  258.9 1.9 copy.136
  260.8 1.9 multiply_reduce_fusion
  262.7 4.8 %convolution_convert_fusion = bf16[256,4096]{1,0:T(8,128)(2,1)} fusion(bf16[256,512]{0,1:T(8,128)(2,1)S(1)} %bitcast.424, bf16[512,4096]{1,0:T(8,128)(2,1)} %all-gather.3.cloned.1.call-done), kind=kOutput, calls=%fused_computation | convolution fusion | flops 1074790400 | bytes 6553600 | tf_op jit(solution)/shard_map/dot_general | solution.py:97
  267.6 1.8 fusion.29
  269.4 1.2 convolution_bitcast_fusion.5
  270.6 1.3 fusion.25
  272.0 0.4 fusion.26
  272.4 0.4 fusion.27
  272.8 0.3 convolution_add_fusion.3
  273.0 0.3 convolution_add_fusion.2
  273.3 0.3 convolution_add_fusion.1
  273.6 0.4 fusion.28
  274.0 1.0 fusion.31
  274.9 1.8 copy.171
  276.8 1.5 fusion.36
  278.2 1.6 fusion.35
  279.8 2.3 collective-permute-start.4
  282.1 1.3 convolution_bitcast_fusion.13
  283.4 1.3 convolution_bitcast_fusion.11
  284.7 0.3 convolution_bitcast_fusion.9
  285.1 0.3 convolution_bitcast_fusion.7
  285.4 0.3 convolution_bitcast_fusion.14
  285.7 0.6 collective-permute-done.4
  286.3 3.0 collective-permute-start.5
  289.3 0.3 convolution_bitcast_fusion.12
  289.6 3.4 collective-permute-done.5
  293.0 1.9 collective-permute-start.6
  295.0 0.3 convolution_bitcast_fusion.10
  295.2 4.5 %collective-permute-done.6 = bf16[2,256,128]{2,1,0:T(8,128)(2,1)S(1)} collective-permute-done((bf16[2,256,128]{2,1,0:T(8,128)(2,1)S(1)}, bf16[2,256,128]{2,1,0:T(8,128)(2,1)S(1)}, u32[]{:S(2)}, u32[]{:S(2)}) %collective-permute-start.6) | collective-permute-done | bytes 131104 | tf_op jit(solution)/shard_map/ppermute | solution.py:18
  299.7 1.9 collective-permute-start.7
  301.7 0.3 convolution_bitcast_fusion.8
  302.0 4.5 %collective-permute-done.7 = bf16[2,256,128]{2,1,0:T(8,128)(2,1)S(1)} collective-permute-done((bf16[2,256,128]{2,1,0:T(8,128)(2,1)S(1)}, bf16[2,256,128]{2,1,0:T(8,128)(2,1)S(1)}, u32[]{:S(2)}, u32[]{:S(2)}) %collective-permute-start.7) | collective-permute-done | bytes 131104 | tf_op jit(solution)/shard_map/ppermute | solution.py:18
  306.5 0.6 fusion.62
  307.1 0.6 fusion.61
  307.7 101.7 %reduce-scatter.2.cloned.1.call-done = bf16[256,512]{1,0:T(8,128)(2,1)} async-done(((bf16[256,4096]{1,0:T(8,128)(2,1)}), bf16[256,512]{1,0:T(8,128)(2,1)}) %reduce-scatter.2.cloned.1.call-update) | async-done | bytes 262160 | tf_op jit(solution)/shard_map/reduce_scatter | solution.py:103
  (87 shorter events, 1.4 us)
Async XLA Ops:
  7.2 8.4 %copy-start = (bf16[256,512]{1,0:T(8,128)(2,1)S(1)}, bf16[256,512]{1,0:T(8,128)(2,1)}, u32[]{:S(2)}) copy-start(bf16[256,512]{1,0:T(8,128)(2,1)} %param.6) | copy-start | bytes 786436
  7.2 121.1 %all-gather.5.cloned.1.call-start = ((), (), s32[]{:S(2)}) async-start(), calls=%async_computation.3 | async-start | bytes 2359296 | tf_op jit(solution)/shard_map/all_gather | solution.py:106
  7.9 244.4 %all-gather.3.cloned.1.call-start = ((), (), s32[]{:S(2)}) async-start(), calls=%async_computation.1 | async-start | bytes 4259840 | tf_op jit(solution)/shard_map/all_gather | solution.py:99
  8.7 400.8 %reduce-scatter.2.cloned.1.call-start = ((), (), s32[]{:S(2)}) async-start(), calls=%async_computation.2 | async-start | bytes 2359296 | tf_op jit(solution)/shard_map/reduce_scatter | solution.py:103
  9.6 7.4 %collective-permute-start = (bf16[2,256,128]{2,1,0:T(8,128)(2,1)S(1)}, bf16[2,256,128]{2,1,0:T(8,128)(2,1)S(1)}, u32[]{:S(2)}, u32[]{:S(2)}) collective-permute-start(bf16[2,256,128]{2,1,0:T(8,128)(2,1)S(1)} %pad_maximum_fusion), channel_id=1, source_target_pairs={{0,8},{8,16},{16,24},{24,32},{32,40},{40,48},{48,56},{56,64},{64,7... | collective-permute-start | bytes 393224 | tf_op jit(solution)/shard_map/ppermute | solution.py:18
  15.5 18.9 %copy-start.18 = (pred[256,256]{0,1:T(8,128)(4,1)}, pred[256,256]{0,1:T(8,128)(4,1)S(1)}, u32[]{:S(2)}) copy-start(pred[256,256]{0,1:T(8,128)(4,1)S(1)} %get-tuple-element.22) | copy-start | bytes 196612
  15.5 20.2 %copy-start.20 = (pred[256,256]{0,1:T(8,128)(4,1)}, pred[256,256]{0,1:T(8,128)(4,1)S(1)}, u32[]{:S(2)}) copy-start(pred[256,256]{0,1:T(8,128)(4,1)S(1)} %get-tuple-element.24) | copy-start | bytes 196612
  15.6 21.2 %copy-start.16 = (pred[256,256]{0,1:T(8,128)(4,1)}, pred[256,256]{0,1:T(8,128)(4,1)S(1)}, u32[]{:S(2)}) copy-start(pred[256,256]{0,1:T(8,128)(4,1)S(1)} %get-tuple-element.25) | copy-start | bytes 196612
  16.8 18.9 %copy-start.3 = (f32[1,4,256,256]{2,3,1,0:T(8,128)}, f32[1,4,256,256]{2,3,1,0:T(8,128)S(1)}, u32[]{:S(2)}) copy-start(f32[1,4,256,256]{2,3,1,0:T(8,128)S(1)} %get-tuple-element.29) | copy-start | bytes 3145732
  17.0 8.9 %copy-start.23 = (bf16[2,256,128]{2,1,0:T(8,128)(2,1)}, bf16[2,256,128]{2,1,0:T(8,128)(2,1)S(1)}, u32[]{:S(2)}) copy-start(bf16[2,256,128]{2,1,0:T(8,128)(2,1)S(1)} %collective-permute-done) | copy-start | bytes 393220
  17.0 4.6 %collective-permute-start.1 = (bf16[2,256,128]{2,1,0:T(8,128)(2,1)S(1)}, bf16[2,256,128]{2,1,0:T(8,128)(2,1)S(1)}, u32[]{:S(2)}, u32[]{:S(2)}) collective-permute-start(bf16[2,256,128]{2,1,0:T(8,128)(2,1)S(1)} %collective-permute-done), channel_id=1, source_target_pairs={{0,8},{8,16},{16,24},{24,32},{32,40},{40,48},{48,56},{56,64},{64,7... | collective-permute-start | bytes 393224 | tf_op jit(solution)/shard_map/ppermute | solution.py:18
  20.0 15.7 %copy-start.22 = (bf16[256,128]{1,0:T(8,128)(2,1)S(1)}, bf16[256,128]{1,0:T(8,128)(2,1)}, u32[]{:S(2)}) copy-start(bf16[256,128]{1,0:T(8,128)(2,1)} %param.8) | copy-start | bytes 196612
  21.6 14.8 %copy-start.26 = (bf16[2,256,128]{2,1,0:T(8,128)(2,1)}, bf16[2,256,128]{2,1,0:T(8,128)(2,1)S(1)}, u32[]{:S(2)}) copy-start(bf16[2,256,128]{2,1,0:T(8,128)(2,1)S(1)} %collective-permute-done.1) | copy-start | bytes 393220
  21.6 6.3 %collective-permute-start.2 = (bf16[2,256,128]{2,1,0:T(8,128)(2,1)S(1)}, bf16[2,256,128]{2,1,0:T(8,128)(2,1)S(1)}, u32[]{:S(2)}, u32[]{:S(2)}) collective-permute-start(bf16[2,256,128]{2,1,0:T(8,128)(2,1)S(1)} %collective-permute-done.1), channel_id=1, source_target_pairs={{0,8},{8,16},{16,24},{24,32},{32,40},{40,48},{48,56},{56,64},{64,7... | collective-permute-start | bytes 393224 | tf_op jit(solution)/shard_map/ppermute | solution.py:18
  26.3 9.8 %copy-start.24 = (bf16[2,256,128]{2,1,0:T(8,128)(2,1)S(1)}, bf16[2,256,128]{2,1,0:T(8,128)(2,1)}, u32[]{:S(2)}) copy-start(bf16[2,256,128]{2,1,0:T(8,128)(2,1)} %copy-done.23) | copy-start | bytes 393220
  27.9 8.9 %copy-start.28 = (bf16[2,256,128]{2,1,0:T(8,128)(2,1)}, bf16[2,256,128]{2,1,0:T(8,128)(2,1)S(1)}, u32[]{:S(2)}) copy-start(bf16[2,256,128]{2,1,0:T(8,128)(2,1)S(1)} %collective-permute-done.2) | copy-start | bytes 393220
  27.9 6.3 %collective-permute-start.3 = (bf16[2,256,128]{2,1,0:T(8,128)(2,1)S(1)}, bf16[2,256,128]{2,1,0:T(8,128)(2,1)S(1)}, u32[]{:S(2)}, u32[]{:S(2)}) collective-permute-start(bf16[2,256,128]{2,1,0:T(8,128)(2,1)S(1)} %collective-permute-done.2), channel_id=1, source_target_pairs={{0,8},{8,16},{16,24},{24,32},{32,40},{40,48},{48,56},{56,64},{64,7... | collective-permute-start | bytes 393224 | tf_op jit(solution)/shard_map/ppermute | solution.py:18
  34.1 2.6 copy-start.30
  34.5 1.0 copy-start.1
  267.5 4.4 %copy-start.5 = (bf16[256,512]{0,1:T(8,128)(2,1)S(1)}, bf16[256,512]{0,1:T(8,128)(2,1)}, u32[]{:S(2)}) copy-start(bf16[256,512]{0,1:T(8,128)(2,1)} %copy.218) | copy-start | bytes 786436
  267.5 4.4 %copy-start.27 = (bf16[2,256,128]{2,1,0:T(8,128)(2,1)S(1)}, bf16[2,256,128]{2,1,0:T(8,128)(2,1)}, u32[]{:S(2)}) copy-start(bf16[2,256,128]{2,1,0:T(8,128)(2,1)} %copy-done.26) | copy-start | bytes 393220
  267.5 4.8 %copy-start.17 = (pred[256,256]{0,1:T(8,128)(4,1)S(1)}, pred[256,256]{0,1:T(8,128)(4,1)}, u32[]{:S(2)}) copy-start(pred[256,256]{0,1:T(8,128)(4,1)} %copy-done.16) | copy-start | bytes 196612
  267.6 4.8 %copy-start.29 = (bf16[2,256,128]{2,1,0:T(8,128)(2,1)S(1)}, bf16[2,256,128]{2,1,0:T(8,128)(2,1)}, u32[]{:S(2)}) copy-start(bf16[2,256,128]{2,1,0:T(8,128)(2,1)} %copy-done.28) | copy-start | bytes 393220
  267.6 5.2 %copy-start.25 = (bf16[2,256,128]{2,1,0:T(8,128)(2,1)S(1)}, bf16[2,256,128]{2,1,0:T(8,128)(2,1)}, u32[]{:S(2)}) copy-start(bf16[2,256,128]{2,1,0:T(8,128)(2,1)} %copy-done.23) | copy-start | bytes 393220
  269.3 1.2 copy-start.13
  271.9 1.6 copy-start.7
  271.9 1.6 copy-start.2
  271.9 1.6 copy-start.19
  272.0 1.6 copy-start.31
  272.4 1.6 copy-start.9
  272.7 2.2 copy-start.11
  273.9 1.0 copy-start.15
  276.7 8.0 %copy-start.6 = (bf16[256,512]{0,1:T(8,128)(2,1)S(1)}, bf16[256,512]{0,1:T(8,128)(2,1)}, u32[]{:S(2)}) copy-start(bf16[256,512]{0,1:T(8,128)(2,1)} %copy.218) | copy-start | bytes 786436
  276.7 8.3 %copy-start.4 = (f32[1,4,256,256]{2,3,1,0:T(8,128)S(1)}, f32[1,4,256,256]{2,3,1,0:T(8,128)}, u32[]{:S(2)}) copy-start(f32[1,4,256,256]{2,3,1,0:T(8,128)} %copy-done.3) | copy-start | bytes 3145732
  276.7 8.3 %copy-start.21 = (pred[256,256]{0,1:T(8,128)(4,1)S(1)}, pred[256,256]{0,1:T(8,128)(4,1)}, u32[]{:S(2)}) copy-start(pred[256,256]{0,1:T(8,128)(4,1)} %copy-done.20) | copy-start | bytes 196612
  276.7 8.7 %copy-start.12 = (bf16[4,256,256]{1,2,0:T(8,128)(2,1)S(1)}, bf16[4,256,256]{1,2,0:T(8,128)(2,1)}, u32[]{:S(2)}) copy-start(bf16[4,256,256]{1,2,0:T(8,128)(2,1)} %copy-done.11) | copy-start | bytes 1572868
  279.8 9.5 %copy-start.10 = (bf16[4,256,256]{1,2,0:T(8,128)(2,1)S(1)}, bf16[4,256,256]{1,2,0:T(8,128)(2,1)}, u32[]{:S(2)}) copy-start(bf16[4,256,256]{1,2,0:T(8,128)(2,1)} %copy-done.9) | copy-start | bytes 1572868
  279.8 15.1 %copy-start.8 = (bf16[4,256,256]{1,2,0:T(8,128)(2,1)S(1)}, bf16[4,256,256]{1,2,0:T(8,128)(2,1)}, u32[]{:S(2)}) copy-start(bf16[4,256,256]{1,2,0:T(8,128)(2,1)} %copy-done.7) | copy-start | bytes 1572868
  279.8 6.4 %collective-permute-start.4 = (bf16[2,256,128]{2,1,0:T(8,128)(2,1)S(1)}, bf16[2,256,128]{2,1,0:T(8,128)(2,1)S(1)}, u32[]{:S(2)}, u32[]{:S(2)}) collective-permute-start(bf16[2,256,128]{2,1,0:T(8,128)(2,1)S(1)} %pad_maximum_fusion.1), channel_id=1, source_target_pairs={{8,0},{16,8},{24,16},{32,24},{40,32},{48,40},{56,48},{64,56},{72,6... | collective-permute-start | bytes 393224 | tf_op jit(solution)/shard_map/ppermute | solution.py:18
  283.4 18.3 %copy-start.14 = (bf16[4,256,256]{1,2,0:T(8,128)(2,1)S(1)}, bf16[4,256,256]{1,2,0:T(8,128)(2,1)}, u32[]{:S(2)}) copy-start(bf16[4,256,256]{1,2,0:T(8,128)(2,1)} %copy-done.13) | copy-start | bytes 1572868
  286.3 6.7 %collective-permute-start.5 = (bf16[2,256,128]{2,1,0:T(8,128)(2,1)S(1)}, bf16[2,256,128]{2,1,0:T(8,128)(2,1)S(1)}, u32[]{:S(2)}, u32[]{:S(2)}) collective-permute-start(bf16[2,256,128]{2,1,0:T(8,128)(2,1)S(1)} %fusion.57), channel_id=1, source_target_pairs={{8,0},{16,8},{24,16},{32,24},{40,32},{48,40},{56,48},{64,56},{72,6... | collective-permute-start | bytes 393224 | tf_op jit(solution)/shard_map/ppermute | solution.py:18
  293.0 6.7 %collective-permute-start.6 = (bf16[2,256,128]{2,1,0:T(8,128)(2,1)S(1)}, bf16[2,256,128]{2,1,0:T(8,128)(2,1)S(1)}, u32[]{:S(2)}, u32[]{:S(2)}) collective-permute-start(bf16[2,256,128]{2,1,0:T(8,128)(2,1)S(1)} %fusion.58), channel_id=1, source_target_pairs={{8,0},{16,8},{24,16},{32,24},{40,32},{48,40},{56,48},{64,56},{72,6... | collective-permute-start | bytes 393224 | tf_op jit(solution)/shard_map/ppermute | solution.py:18
  299.7 6.7 %collective-permute-start.7 = (bf16[2,256,128]{2,1,0:T(8,128)(2,1)S(1)}, bf16[2,256,128]{2,1,0:T(8,128)(2,1)S(1)}, u32[]{:S(2)}, u32[]{:S(2)}) collective-permute-start(bf16[2,256,128]{2,1,0:T(8,128)(2,1)S(1)} %fusion.59), channel_id=1, source_target_pairs={{8,0},{16,8},{24,16},{32,24},{40,32},{48,40},{56,48},{64,56},{72,6... | collective-permute-start | bytes 393224 | tf_op jit(solution)/shard_map/ppermute | solution.py:18
Sparse Core Ops, SparseCore 0:
  11.1 117.2 all-gather.4
  130.5 121.7 all-gather.2
  267.6 141.7 reduce-scatter.1
where the time goes:
time: 418 us; the launch traced here: 416 us
  waiting for transfers between devices  334 us (80%)
  matrix products  30.6 us (7%)
  starting transfers between devices  24.3 us (6%)
  between operations  14.5 us (3%)
  local copies, waits for them, and re-layouts  8 us (2%)
    all_gather x1, waiting for transfers between devices, local(): lax.all_gather(out_weight, 'seq', axis=0, tiled=True)  124 us
    reduce_scatter x1, waiting for transfers between devices, local(): lax.psum_scatter(rounded.astype(jnp.bfloat16), 'tensor', scatter_dimensio...  102 us
    all_gather x1, waiting for transfers between devices, local(): grad_rows = lax.all_gather(out_grad, 'tensor', axis=1, tiled=True)  90.4 us
    ppermute x8, starting transfers between devices, shifted(): lax.ppermute(value, axis, [(source, source + steps) for source in range(l...  24.1 us
    ppermute x8, waiting for transfers between devices, shifted(): lax.ppermute(value, axis, [(source, source + steps) for source in range(l...  17 us
  transfers between devices with their start and end apart: 11, of which 10 were waited for; matrix products, arithmetic and copies ran while one was open for 6% of the time, Pallas kernels for 0%

commit v1 on v0

v1 whole, which is shorter than its diff:
```python
import math

import jax
import jax.numpy as jnp
from jax import lax
from jax.experimental import pallas as pl
from jax.experimental.pallas import tpu as pltpu
from jax.sharding import PartitionSpec as P

DH = 128
SPAN = 4
NZ, NY, NX = 8, 4, 4
HEADS = 4
TOK = 256
WIDTH = HEADS * DH
KEYS = (SPAN + 1) * TOK
HALF = NX * WIDTH
CHUNK = 256
SPLIT = WIDTH // CHUNK
ROWS = 2
NEG_FILL = -1e30

MESH = pl.DeviceIdType.MESH
BF = jnp.bfloat16
F32 = jnp.float32
LAST = (((1,), (1,)), ((), ()))
SCALE = 1.0 / math.sqrt(DH)


def aligned(value, step):
    return pl.multiple_of(value * step, step)


def remote(src, dst, send, recv, to):
    return pltpu.make_async_remote_copy(
        src_ref=src, dst_ref=dst, send_sem=send, recv_sem=recv, device_id=to, device_id_type=MESH
    )


def kernel(
    q_hbm, k_hbm, v_hbm, w_ref, og_hbm, len_ref,
    out_hbm, gq_hbm, gk_hbm, gv_hbm,
    q_s, kv_s, vt_s, kt_s, bias_s, s_s, p_s, ctx_s, ctxf_s,
    w_s, wout_s, win_s, g_s, acc_s, gh_s, ds_s, dq_s, delta_s,
    rs_out, rs_in, rs_own, zsum_s, zin_s, attn_s, gq_s,
    dkv_out, dkv_in, dkv_own, gkv_s,
    load_sem, store_sem, sib_sem, kv_ss, kv_rs, z_ss, z_rs, y_ss, y_rs, d_ss, d_rs,
    ox_ss, ox_rs, oz_ss, oz_rs, of_ss, of_rs, rs_ss, rs_rs, rz_ss, rz_rs, gr_ss, gr_rs,
):
    seq = lax.axis_index("seq")
    ten = lax.axis_index("tensor")
    core = lax.rem(seq, 2)
    chip = lax.div(seq, 2)
    y = lax.rem(chip, NY)
    zl = lax.div(chip, NY)
    x = lax.rem(ten, NX)
    zh = lax.div(ten, NX)
    away = 1 - zh
    seqs = 2 * NY * NZ

    def at_x(d):
        return (seq, zh * NX + lax.rem(x + d, NX))

    def at_y(d):
        return ((zl * NY + lax.rem(y + d, NY)) * 2 + core, ten)

    sibling = (chip * 2 + (1 - core), ten)
    partner = (seq, away * NX + x)

    loads = [
        pltpu.make_async_copy(k_hbm, kv_s.at[0, pl.ds(SPAN * TOK, TOK)], load_sem.at[0]),
        pltpu.make_async_copy(v_hbm, kv_s.at[1, pl.ds(SPAN * TOK, TOK)], load_sem.at[1]),
        pltpu.make_async_copy(og_hbm, g_s.at[ten], load_sem.at[2]),
    ] + [
        pltpu.make_async_copy(
            q_hbm.at[:, pl.ds(i * DH, DH)], q_s.at[pl.ds(i * TOK, TOK)], load_sem.at[3 + i]
        )
        for i in range(HEADS)
    ]
    for copy in loads:
        copy.start()

    barrier = pltpu.get_barrier_semaphore()

    def greet(to):
        pl.semaphore_signal(barrier, inc=1, device_id=to, device_id_type=MESH)

    expected = 1 + (NY - 1) + (NX - 1) + 1
    greet(sibling)
    greet(partner)
    for d in range(1, NY):
        greet(at_y(d))
    for d in range(1, NX):
        greet(at_x(d))
    up_ok = zl < NZ - 1
    down_ok = zl > 0

    @pl.when(up_ok)
    def _():
        greet((seq + 2 * NY, ten))

    @pl.when(down_ok)
    def _():
        greet((seq - 2 * NY, ten))

    expected = expected + up_ok.astype(jnp.int32) + down_ok.astype(jnp.int32)
    for d in range(1, SPAN + 1):
        ahead, behind = seq + d < seqs, seq >= d

        @pl.when(ahead)
        def _():
            greet((seq + d, ten))

        @pl.when(behind)
        def _():
            greet((seq - d, ten))

        @pl.when(jnp.logical_not(ahead))
        def _():
            dkv_in[d - 1] = jnp.zeros((2, TOK, DH), BF)

        @pl.when(jnp.logical_not(behind))
        def _():
            kv_s[:, (SPAN - d) * TOK : (SPAN - d + 1) * TOK, :] = jnp.zeros((2, TOK, DH), BF)

        expected = expected + ahead.astype(jnp.int32) + behind.astype(jnp.int32)

    mine = w_ref[:, pl.ds(aligned(core, HALF), HALF)].astype(F32)
    other = w_ref[:, pl.ds(aligned(1 - core, HALF), HALF)].astype(F32)
    wout_s[...] = jnp.concatenate([other[:, : HALF // 2], other[:, HALF // 2 :]], axis=0).astype(BF)

    lengths = len_ref[...]
    docs = lengths.shape[1]
    row = lax.broadcasted_iota(jnp.int32, (docs, docs), 0)
    col = lax.broadcasted_iota(jnp.int32, (docs, docs), 1)
    ends = jnp.sum(jnp.where(col <= row, jnp.broadcast_to(lengths, (docs, docs)), 0), axis=1, keepdims=True)
    place = seq * TOK + lax.broadcasted_iota(jnp.int32, (1, TOK), 1)
    first = jnp.max(jnp.where(ends <= place, ends, 0), axis=0, keepdims=True)
    for e in range(SPAN + 1):
        key_place = (seq - SPAN + e) * TOK + lax.broadcasted_iota(jnp.int32, (TOK, TOK), 0)
        seen = (key_place >= first) & (key_place <= place)
        bias_s[e * TOK : (e + 1) * TOK, :] = jnp.where(seen, 0.0, NEG_FILL)

    pl.semaphore_wait(barrier, expected)

    sib_copy = remote(wout_s, win_s, sib_sem.at[0], sib_sem.at[1], sibling)
    sib_copy.start()

    def kv_copy(d, i, to):
        return remote(
            (k_hbm, v_hbm)[i], kv_s.at[i, pl.ds((SPAN - d) * TOK, TOK)],
            kv_ss.at[d - 1, i], kv_rs.at[d - 1, i], to,
        )

    for d in range(1, SPAN + 1):

        @pl.when(seq + d < seqs)
        def _():
            for i in range(2):
                kv_copy(d, i, (seq + d, ten)).start()

    def ox_copy(d, place):
        return remote(og_hbm, g_s.at[place], ox_ss.at[d - 1], ox_rs.at[d - 1], at_x(d))

    for d in range(1, NX):
        ox_copy(d, ten).start()

    def w_rows(z, yy):
        return w_s.at[core, pl.ds(aligned(z * NY + yy, 16), 16)]

    def z_copy(way, hop, z):
        to = (seq + 2 * NY, ten) if way == 0 else (seq - 2 * NY, ten)
        return remote(w_rows(z, y), w_rows(z, y), z_ss.at[way, hop], z_rs.at[way, hop], to)

    def y_copy(d, z, yy):
        return remote(w_rows(z, yy), w_rows(z, yy), y_ss.at[d - 1, z], y_rs.at[d - 1, z], at_y(d))

    def d_copy(z, half):
        rows = w_s.at[half, pl.ds(aligned(z, NY * 16), NY * 16)]
        return remote(rows, rows, d_ss.at[z], d_rs.at[z], sibling)

    sib_copy.wait_recv()
    came = win_s[...].astype(F32)
    came = jnp.concatenate([came[:8], came[8:]], axis=1)
    upper = jnp.where(core == 0, mine, came)
    lower = jnp.where(core == 0, came, mine)
    w_s[core, pl.ds(aligned(chip, 16), 16), :] = jnp.concatenate([upper, lower], axis=0).astype(BF)

    @pl.when(up_ok)
    def _():
        z_copy(0, 0, zl).start()

    @pl.when(down_ok)
    def _():
        z_copy(1, 0, zl).start()

    for d in range(1, NY):
        y_copy(d, zl, y).start()

    def z_step(hop, carry):
        below, above = zl - hop, zl + hop

        @pl.when(below >= 0)
        def _():
            z_copy(0, hop - 1, below).wait_recv()

            @pl.when(up_ok)
            def _():
                z_copy(0, hop, below).start()

            for d in range(1, NY):
                y_copy(d, below, y).start()

        @pl.when(above < NZ)
        def _():
            z_copy(1, hop - 1, above).wait_recv()

            @pl.when(down_ok)
            def _():
                z_copy(1, hop, above).start()

            for d in range(1, NY):
                y_copy(d, above, y).start()

        return carry

    lax.fori_loop(1, NZ, z_step, 0)

    def oz_copy(i, place):
        rows = pl.ds(i * (TOK // ROWS), TOK // ROWS)
        return remote(og_hbm.at[rows], g_s.at[place, rows], oz_ss.at[i], oz_rs.at[i], partner)

    def of_copy(i, d, place):
        rows = g_s.at[place, pl.ds(i * (TOK // ROWS), TOK // ROWS)]
        return remote(rows, rows, of_ss.at[i, d - 1], of_rs.at[i, d - 1], at_x(d))

    for i in range(ROWS):
        oz_copy(i, ten).start()

    for copy in loads:
        copy.wait()
    for d in range(1, SPAN + 1):

        @pl.when(seq >= d)
        def _():
            for i in range(2):
                kv_copy(d, i, (seq, ten)).wait_recv()

    blocks = [slice(e * TOK, (e + 1) * TOK) for e in range(SPAN + 1)]
    for rows in blocks:
        kt_s[:, rows] = jnp.transpose(kv_s[0, rows, :].astype(F32)).astype(BF)
        vt_s[:, rows] = jnp.transpose(kv_s[1, rows, :].astype(F32)).astype(BF)

    def pass_on(z):
        for d in range(1, NY):
            y_copy(d, z, lax.rem(y + NY - d, NY)).wait_recv()
        d_copy(z, core).start()

    def attend(head, carry):
        lanes = pl.ds(aligned(head, TOK), TOK)
        q = q_s[lanes, :]
        top = jnp.full((1, TOK), NEG_FILL, F32)
        for rows in blocks:
            scores = (
                lax.dot_general(kv_s[0, rows, :], q, LAST, preferred_element_type=F32) * SCALE
                + bias_s[rows, :]
            )
            s_s[rows, :] = scores
            top = jnp.maximum(top, jnp.max(scores, axis=0, keepdims=True))
        total = jnp.zeros((1, TOK), F32)
        for rows in blocks:
            raised = jnp.exp(s_s[rows, :] - top)
            s_s[rows, :] = raised
            total = total + jnp.sum(raised, axis=0, keepdims=True)
        inverse = 1.0 / total
        context = jnp.zeros((DH, TOK), F32)
        for rows in blocks:
            weights = (s_s[rows, :] * inverse).astype(BF)
            p_s[rows, lanes] = weights
            context = context + jnp.dot(vt_s[:, rows], weights, preferred_element_type=F32)
        ctx_s[:, pl.ds(aligned(head, DH), DH)] = jnp.transpose(context).astype(BF)
        for k in (2 * head, 2 * head + 1):

            @pl.when(zl - k >= 0)
            def _():
                pass_on(zl - k)

            @pl.when((k > 0) & (zl + k < NZ))
            def _():
                pass_on(zl + k)

        return carry

    lax.fori_loop(0, HEADS, attend, 0)
    for z in range(NZ):
        d_copy(z, 1 - core).wait_recv()

    def rs_copy(side, place, d):
        return remote(
            rs_out.at[side, place], rs_in.at[side, place],
            rs_ss.at[side, place], rs_rs.at[side, place], at_x(d),
        )

    def share(half, xx, j):
        lanes = pl.ds(aligned(xx * SPLIT + j, CHUNK), CHUNK)
        return jnp.dot(ctx_s[...], w_s[half, :, lanes], preferred_element_type=F32).astype(BF)

    def project(side, half):
        def step(place, carry):
            d, j = lax.rem(place, NX - 1) + 1, lax.div(place, NX - 1)
            rs_out[side, place] = share(half, lax.rem(x + d, NX), j)
            rs_copy(side, place, d).start()
            return carry

        lax.fori_loop(0, SPLIT * (NX - 1), step, 0)

        def own(j, carry):
            rs_own[side, j] = share(half, x, j)
            return carry

        lax.fori_loop(0, SPLIT, own, 0)

    def collect(side, j):
        total = rs_own[side, j].astype(F32)
        for d in range(1, NX):
            place = j * (NX - 1) + d - 1
            rs_copy(side, place, d).wait_recv()
            total = total + rs_in[side, place].astype(F32)
        return total

    project(0, away)

    def rz_copy(j):
        return remote(zsum_s.at[j], zin_s.at[j], rz_ss.at[j], rz_rs.at[j], partner)

    def og_forward(i):
        oz_copy(i, away * NX + x).wait_recv()
        for d in range(1, NX):
            of_copy(i, d, away * NX + x).start()

    project(1, zh)
    og_forward(0)
    for j in range(SPLIT):
        zsum_s[j] = collect(0, j).astype(BF)
        rz_copy(j).start()
    for i in range(1, ROWS):
        og_forward(i)

    def grad_part(half):
        def step(xx, carry):
            lanes = pl.ds(aligned(xx, WIDTH), WIDTH)
            acc_s[...] += lax.dot_general(
                g_s[half * NX + xx], w_s[half, :, lanes], LAST, preferred_element_type=F32
            )
            return carry

        lax.fori_loop(0, NX, step, 0)

    acc_s[...] = jnp.zeros_like(acc_s)
    for d in range(1, NX):
        ox_copy(d, zh * NX + lax.rem(x + NX - d, NX)).wait_recv()
    grad_part(zh)
    for i in range(ROWS):
        for d in range(1, NX):
            of_copy(i, d, away * NX + lax.rem(x + NX - d, NX)).wait_recv()
    grad_part(away)

    for i in range(HEADS):
        grad = acc_s[:, i * DH : (i + 1) * DH].astype(BF)
        gh_s[i * TOK : (i + 1) * TOK, :] = grad
        product = grad.astype(F32) * ctx_s[:, i * DH : (i + 1) * DH].astype(F32)
        delta_s[:, i * TOK : (i + 1) * TOK] = jnp.sum(jnp.transpose(product), axis=0, keepdims=True)

    def gr_copy(d, to):
        return remote(dkv_out.at[d - 1], dkv_in.at[d - 1], gr_ss.at[d - 1], gr_rs.at[d - 1], to)

    dq_s[...] = jnp.zeros_like(dq_s)
    for e, rows in enumerate(blocks):
        d = SPAN - e
        values = kv_s[1, rows, :]

        def back(head, carry):
            lanes = pl.ds(aligned(head, TOK), TOK)
            slope = lax.dot_general(values, gh_s[lanes, :], LAST, preferred_element_type=F32)
            ds_s[:, lanes] = (p_s[rows, lanes].astype(F32) * (slope - delta_s[:, lanes])).astype(BF)
            dq_s[:, lanes] += jnp.dot(kt_s[:, rows], ds_s[:, lanes], preferred_element_type=F32)
            return carry

        lax.fori_loop(0, HEADS, back, 0)
        dk = jnp.dot(ds_s[...], q_s[...], preferred_element_type=F32)
        dv = jnp.dot(p_s[rows, :], gh_s[...], preferred_element_type=F32)
        if d == 0:
            dkv_own[0] = dk
            dkv_own[1] = dv
        else:
            dkv_out[d - 1, 0] = dk.astype(BF)
            dkv_out[d - 1, 1] = dv.astype(BF)

            @pl.when(seq >= d)
            def _():
                gr_copy(d, (seq - d, ten)).start()

    for i in range(HEADS):
        gq_s[:, i * DH : (i + 1) * DH] = (
            jnp.transpose(dq_s[:, i * TOK : (i + 1) * TOK]) * SCALE
        ).astype(BF)
    stores = [pltpu.make_async_copy(gq_s, gq_hbm, store_sem.at[0])]
    stores[0].start()

    for j in range(SPLIT):
        total = collect(1, j)
        rz_copy(j).wait_recv()
        lanes = slice(j * CHUNK, (j + 1) * CHUNK)
        attn_s[:, lanes] = (total + zin_s[j].astype(F32)).astype(BF)
    stores.append(pltpu.make_async_copy(attn_s, out_hbm, store_sem.at[1]))
    stores[1].start()

    for d in range(1, SPAN + 1):

        @pl.when(seq + d < seqs)
        def _():
            gr_copy(d, (seq, ten)).wait_recv()

    for i in range(2):
        total = dkv_own[i]
        for d in range(1, SPAN + 1):
            total = total + dkv_in[d - 1, i].astype(F32)
        gkv_s[i] = ((total * SCALE) if i == 0 else total).astype(BF)
        stores.append(
            pltpu.make_async_copy(gkv_s.at[i], (gk_hbm, gv_hbm)[i], store_sem.at[2 + i])
        )
        stores[-1].start()

    sib_copy.wait_send()
    for d in range(1, SPAN + 1):

        @pl.when(seq + d < seqs)
        def _():
            for i in range(2):
                kv_copy(d, i, (seq, ten)).wait_send()

        @pl.when(seq >= d)
        def _():
            gr_copy(d, (seq, ten)).wait_send()

    for d in range(1, NX):
        ox_copy(d, ten).wait_send()
        for i in range(ROWS):
            of_copy(i, d, away * NX + x).wait_send()
    for i in range(ROWS):
        oz_copy(i, ten).wait_send()

    def drain(z, carry):
        for d in range(1, NY):
            y_copy(d, z, y).wait_send()
        d_copy(z, core).wait_send()

        @pl.when((z <= zl) & up_ok)
        def _():
            z_copy(0, z, zl).wait_send()

        @pl.when((z < NZ - zl) & down_ok)
        def _():
            z_copy(1, z, zl).wait_send()

        return carry

    lax.fori_loop(0, NZ, drain, 0)
    for side in range(2):
        for place in range(SPLIT * (NX - 1)):
            rs_copy(side, place, 1).wait_send()
    for j in range(SPLIT):
        rz_copy(j).wait_send()
    for copy in stores:
        copy.wait()


def local(queries, key_rows, value_rows, out_weight, out_grad, doc_lengths):
    anywhere = pl.BlockSpec(memory_space=pl.ANY)
    vmem = pl.BlockSpec(memory_space=pltpu.VMEM)
    dma = pltpu.SemaphoreType.DMA
    places = SPLIT * (NX - 1)
    scratch = [
        ((HEADS * TOK, DH), BF), ((2, KEYS, DH), BF), ((DH, KEYS), BF), ((DH, KEYS), BF),
        ((KEYS, TOK), F32), ((KEYS, TOK), F32), ((KEYS, HEADS * TOK), BF),
        ((TOK, WIDTH), BF), ((8, 128), F32),
        ((2, WIDTH, HALF), BF), ((16, HALF // 2), BF), ((16, HALF // 2), BF),
        ((2 * NX, TOK, WIDTH), BF), ((TOK, WIDTH), F32), ((HEADS * TOK, DH), BF),
        ((TOK, HEADS * TOK), BF), ((DH, HEADS * TOK), F32), ((1, HEADS * TOK), F32),
        ((2, places, TOK, CHUNK), BF), ((2, places, TOK, CHUNK), BF), ((2, SPLIT, TOK, CHUNK), BF),
        ((SPLIT, TOK, CHUNK), BF), ((SPLIT, TOK, CHUNK), BF), ((TOK, WIDTH), BF), ((TOK, WIDTH), BF),
        ((SPAN, 2, TOK, DH), BF), ((SPAN, 2, TOK, DH), BF), ((2, TOK, DH), F32), ((2, TOK, DH), BF),
    ]
    semaphores = [
        (3 + HEADS,), (4,), (2,), (SPAN, 2), (SPAN, 2), (2, NZ), (2, NZ), (NY - 1, NZ), (NY - 1, NZ),
        (NZ,), (NZ,), (NX - 1,), (NX - 1,), (ROWS,), (ROWS,), (ROWS, NX - 1), (ROWS, NX - 1),
        (2, places), (2, places), (SPLIT,), (SPLIT,), (SPAN,), (SPAN,),
    ]
    return pl.pallas_call(
        kernel,
        name="attention_block",
        out_shape=[
            jax.ShapeDtypeStruct(queries.shape, BF),
            jax.ShapeDtypeStruct(queries.shape, BF),
            jax.ShapeDtypeStruct(key_rows.shape, BF),
            jax.ShapeDtypeStruct(value_rows.shape, BF),
        ],
        in_specs=[anywhere, anywhere, anywhere, vmem, anywhere, vmem],
        out_specs=[anywhere] * 4,
        scratch_shapes=[pltpu.VMEM(shape, kind) for shape, kind in scratch]
        + [dma(shape) for shape in semaphores],
        compiler_params=pltpu.CompilerParams(
            collective_id=0, has_side_effects=True, vmem_limit_bytes=48 * 2**20
        ),
        cost_estimate=pl.CostEstimate(
            flops=5 * 10**9, bytes_accessed=2 * 10**6, transcendentals=1400000
        ),
    )(queries, key_rows, value_rows, out_weight, out_grad, doc_lengths.reshape(1, -1))


def solution(mesh):
    placed = (
        P("seq", "tensor"),
        P("seq", "tensor"),
        P("seq", "tensor"),
        P(("tensor", "seq"), None),
        P("seq", "tensor"),
        P(),
    )
    return jax.shard_map(
        local,
        mesh=mesh,
        in_specs=placed,
        out_specs=(P("seq", "tensor"), P("seq", "tensor"), P("seq", "tensor"), P("seq", "tensor")),
        check_vma=False,
    )
```

time: 418 us -> 136 us (0.33)
  waiting for transfers between devices: 334 us -> 0 us
  Pallas kernels: 0 us -> 127 us
  matrix products: 30.6 us -> 0 us
  starting transfers between devices: 24.3 us -> 0 us
  between operations: 14.5 us -> 0.66 us
    all_gather x2 -> x0, waiting for transfers between devices: 214 us -> none  [the longest x1 124 us: local(): lax.all_gather(out_weight, 'seq', axis=0, tiled=True)]
    pallas_call x0 -> x1, Pallas kernels: none -> 127 us  [local(): pl.pallas_call(kernel, name='attention_block', out_shape=[jax.ShapeDtypeS...]
    reduce_scatter x1 -> x0, waiting for transfers between devices: 102 us -> none  [local(): lax.psum_scatter(rounded.astype(jnp.bfloat16), 'tensor', scatter_dimensio...]
    dot_general x32 -> x0, matrix products: 30.6 us -> none  [the longest x1 4.82 us: local(): lax.dot_general(grad_rows, lax.all_gather(out_weight, 'seq', axis=0, tile...]
    ppermute x8 -> x0, starting transfers between devices: 24.1 us -> none  [shifted(): lax.ppermute(value, axis, [(source, source + steps) for source in range(l...]
    ppermute x8 -> x0, waiting for transfers between devices: 17 us -> none  [shifted(): lax.ppermute(value, axis, [(source, source + steps) for source in range(l...]
    unnamed x65 -> x16, local copies, waits for them, and re-layouts: 2.91 us -> 7.73 us
  transfers between devices with their start and end apart: 11 -> 0, of which waited for: 10 -> 0; matrix products, arithmetic and copies ran while one was open for 6% -> 0% of each run, Pallas kernels for 0% -> 0%
where the time goes in v1:
time: 136 us
  Pallas kernels  127 us (93%)
  local copies, waits for them, and re-layouts  7.73 us (6%)
    pallas_call x1, Pallas kernels, local(): pl.pallas_call(kernel, name='attention_block', out_shape=[jax.ShapeDtypeS...  127 us
    unnamed x16, local copies, waits for them, and re-layouts  7.73 us

profile of v1, /device:TPU:9, one launch (start us, length us, event | category | flops | bytes accessed | tf_op | source)
XLA Modules:
  0.0 135.5 jit_solution(6157783324974265805)
XLA Ops:
  0.6 0.0 copy-start.5
  0.6 0.6 copy-done.5
  1.3 0.0 copy-start
  1.3 0.9 copy-done
  2.2 0.0 copy-start.1
  2.2 0.9 copy-done.1
  3.2 0.0 copy-start.2
  3.2 0.8 copy-done.2
  4.0 0.0 copy-start.3
  4.0 0.8 copy-done.3
  4.9 0.0 copy-start.4
  4.9 0.8 copy-done.4
  5.7 127.1 %attention_block.1 = (bf16[256,512]{1,0:T(8,128)(2,1)S(1)}, bf16[256,512]{1,0:T(8,128)(2,1)S(1)}, bf16[256,128]{1,0:T(8,128)(2,1)S(1)}, bf16[256,128]{1,0:T(8,128)(2,1)S(1)}) custom-call(bf16[256,512]{1,0:T(8,128)(2,1)S(1)} %copy-done, bf16[256,128]{1,0:T(8,128)(2,1)S(1)} %copy-done.2, bf16[256,128]{1,0:T(8,128)(2,1)S(1)} %copy-done.3, ...), custom_call_target="tpu_custom_call" | custom-call | flops 5000000000 | bytes 2000000 | tf_op jit(solution)/shard_map/attention_block/pallas_call | solution.py:499
  132.8 0.7 copy.14
  133.5 0.7 copy.15
  134.3 0.6 copy.16
  134.9 0.6 copy.17
Async XLA Ops:
  0.6 0.7 copy-start.5
  1.3 0.9 copy-start
  2.2 0.9 copy-start.1
  3.2 0.8 copy-start.2
  4.0 0.8 copy-start.3
  4.9 0.8 copy-start.4

commit v2 on v1

--- a/solution.py
+++ b/solution.py
@@ -17,7 +17,8 @@
 HALF = NX * WIDTH
 CHUNK = 256
 SPLIT = WIDTH // CHUNK
-ROWS = 2
+PARTS = 8
+EARLY = 4
 NEG_FILL = -1e30
 
 MESH = pl.DeviceIdType.MESH
@@ -40,11 +41,11 @@
 def kernel(
     q_hbm, k_hbm, v_hbm, w_ref, og_hbm, len_ref,
     out_hbm, gq_hbm, gk_hbm, gv_hbm,
-    q_s, kv_s, vt_s, kt_s, bias_s, s_s, p_s, ctx_s, ctxf_s,
-    w_s, wout_s, win_s, g_s, acc_s, gh_s, ds_s, dq_s, delta_s,
+    q_s, kv_s, vt_s, kt_s, bias_s, s_s, p_s, ctx_s,
+    w_s, wout_s, win_s, g_s, acc_s, gh_s, ds_s, delta_s,
     rs_out, rs_in, rs_own, zsum_s, zin_s, attn_s, gq_s,
     dkv_out, dkv_in, dkv_own, gkv_s,
-    load_sem, store_sem, sib_sem, kv_ss, kv_rs, z_ss, z_rs, y_ss, y_rs, d_ss, d_rs,
+    load_sem, store_sem, sib_sem, kv_ss, kv_rs, ks_ss, ks_rs, z_ss, z_rs, y_ss, y_rs, d_ss, d_rs,
     ox_ss, ox_rs, oz_ss, oz_rs, of_ss, of_rs, rs_ss, rs_rs, rz_ss, rz_rs, gr_ss, gr_rs,
 ):
     seq = lax.axis_index("seq")
@@ -141,29 +142,47 @@
         seen = (key_place >= first) & (key_place <= place)
         bias_s[e * TOK : (e + 1) * TOK, :] = jnp.where(seen, 0.0, NEG_FILL)
 
+    for copy in loads[:2]:
+        copy.wait()
     pl.semaphore_wait(barrier, expected)
 
     sib_copy = remote(wout_s, win_s, sib_sem.at[0], sib_sem.at[1], sibling)
     sib_copy.start()
 
-    def kv_copy(d, i, to):
-        return remote(
-            (k_hbm, v_hbm)[i], kv_s.at[i, pl.ds((SPAN - d) * TOK, TOK)],
-            kv_ss.at[d - 1, i], kv_rs.at[d - 1, i], to,
-        )
-
-    for d in range(1, SPAN + 1):
-
-        @pl.when(seq + d < seqs)
-        def _():
-            for i in range(2):
-                kv_copy(d, i, (seq + d, ten)).start()
-
     def ox_copy(d, place):
         return remote(og_hbm, g_s.at[place], ox_ss.at[d - 1], ox_rs.at[d - 1], at_x(d))
 
     for d in range(1, NX):
         ox_copy(d, ten).start()
+
+    def oz_copy(i, place):
+        rows = pl.ds(aligned(i, TOK // PARTS), TOK // PARTS)
+        return remote(og_hbm.at[rows], g_s.at[place, rows], oz_ss.at[i], oz_rs.at[i], partner)
+
+    def of_copy(i, d, place):
+        rows = g_s.at[place, pl.ds(aligned(i, TOK // PARTS), TOK // PARTS)]
+        return remote(rows, rows, of_ss.at[i, d - 1], of_rs.at[i, d - 1], at_x(d))
+
+    def og_forward(i, carry=0):
+        oz_copy(i, away * NX + x).wait_recv()
+        for d in range(1, NX):
+            of_copy(i, d, away * NX + x).start()
+        return carry
+
+    def kv_rows(e):
+        return kv_s.at[:, pl.ds(aligned(e, TOK), TOK)]
+
+    def kv_copy(n, to):
+        return remote(kv_rows(SPAN), kv_rows(SPAN - 2 * n), kv_ss.at[n - 1], kv_rs.at[n - 1], to)
+
+    def ks_copy(n):
+        return remote(
+            kv_rows(SPAN - 2 * n + 2 - 2 * core), kv_rows(SPAN - 2 * n + 1),
+            ks_ss.at[n - 1], ks_rs.at[n - 1], sibling,
+        )
+
+    def ks_sent(n):
+        return seq >= 2 * n - 2 + 2 * core
 
     def w_rows(z, yy):
         return w_s.at[core, pl.ds(aligned(z * NY + yy, 16), 16)]
@@ -196,8 +215,13 @@
 
     for d in range(1, NY):
         y_copy(d, zl, y).start()
-
-    def z_step(hop, carry):
+    for n in range(1, SPAN // 2 + 1):
+
+        @pl.when(seq + 2 * n < seqs)
+        def _():
+            kv_copy(n, (seq + 2 * n, ten)).start()
+
+    def z_step(hop):
         below, above = zl - hop, zl + hop
 
         @pl.when(below >= 0)
@@ -208,9 +232,6 @@
             def _():
                 z_copy(0, hop, below).start()
 
-            for d in range(1, NY):
-                y_copy(d, below, y).start()
-
         @pl.when(above < NZ)
         def _():
             z_copy(1, hop - 1, above).wait_recv()
@@ -219,81 +240,120 @@
             def _():
                 z_copy(1, hop, above).start()
 
+        @pl.when(below >= 0)
+        def _():
+            for d in range(1, NY):
+                y_copy(d, below, y).start()
+
+        @pl.when(above < NZ)
+        def _():
             for d in range(1, NY):
                 y_copy(d, above, y).start()
 
-        return carry
-
-    lax.fori_loop(1, NZ, z_step, 0)
-
-    def oz_copy(i, place):
-        rows = pl.ds(i * (TOK // ROWS), TOK // ROWS)
-        return remote(og_hbm.at[rows], g_s.at[place, rows], oz_ss.at[i], oz_rs.at[i], partner)
-
-    def of_copy(i, d, place):
-        rows = g_s.at[place, pl.ds(i * (TOK // ROWS), TOK // ROWS)]
-        return remote(rows, rows, of_ss.at[i, d - 1], of_rs.at[i, d - 1], at_x(d))
-
-    for i in range(ROWS):
+    blocks = [slice(e * TOK, (e + 1) * TOK) for e in range(SPAN + 1)]
+
+    def share_keys():
+        for n in range(1, SPAN // 2 + 1):
+
+            @pl.when(seq >= 2 * n)
+            def _():
+                kv_copy(n, (seq, ten)).wait_recv()
+
+        for n in range(1, SPAN // 2 + 1):
+
+            @pl.when(ks_sent(n))
+            def _():
+                ks_copy(n).start()
+
+    def turn_keys():
+        for n in range(1, SPAN // 2 + 1):
+
+            @pl.when(seq >= 2 * n - 1)
+            def _():
+                ks_copy(n).wait_recv()
+
+        for rows in blocks:
+            kt_s[:, rows] = jnp.transpose(kv_s[0, rows, :].astype(F32)).astype(BF)
+            vt_s[:, rows] = jnp.transpose(kv_s[1, rows, :].astype(F32)).astype(BF)
+
+    def attend(heads):
+        lanes = [slice(head * TOK, (head + 1) * TOK) for head in heads]
+        pair = range(len(heads))
+        top = [jnp.full((1, TOK), NEG_FILL, F32)] * len(heads)
+        for rows in blocks:
+            for u in pair:
+                scores = (
+                    lax.dot_general(
+                        kv_s[0, rows, :], q_s[lanes[u], :], LAST, preferred_element_type=F32
+                    )
+                    * SCALE
+                    + bias_s[rows, :]
+                )
+                s_s[u, rows, :] = scores
+                top[u] = jnp.maximum(top[u], jnp.max(scores, axis=0, keepdims=True))
+        total = [jnp.zeros((1, TOK), F32)] * len(heads)
+        for rows in blocks:
+            for u in pair:
+                raised = jnp.exp(s_s[u, rows, :] - top[u])
+                s_s[u, rows, :] = raised
+                total[u] = total[u] + jnp.sum(raised, axis=0, keepdims=True)
+        inverse = [1.0 / each for each in total]
+        context = [jnp.zeros((DH, TOK), F32)] * len(heads)
+        for rows in blocks:
+            for u in pair:
+                weights = (s_s[u, rows, :] * inverse[u]).astype(BF)
+                p_s[rows, lanes[u]] = weights
+                context[u] = context[u] + jnp.dot(
+                    vt_s[:, rows], weights, preferred_element_type=F32
+                )
+        for u in pair:
+            ctx_s[:, heads[u] * DH : (heads[u] + 1) * DH] = jnp.transpose(context[u]).astype(BF)
+
+    oz_copy(0, ten).start()
+    for hop in range(1, NZ):
+        z_step(hop)
+        if hop in (2, 4, 6):
+            oz_copy(hop // 2, ten).start()
+        if hop == 3:
+            share_keys()
+        if hop == 4:
+            for copy in loads[2:]:
+                copy.wait()
+            turn_keys()
+        if hop == 5:
+            attend((0, 1))
+        if hop == 6:
+            attend((2, 3))
+    for i in range(EARLY, PARTS):
         oz_copy(i, ten).start()
-
-    for copy in loads:
-        copy.wait()
-    for d in range(1, SPAN + 1):
-
-        @pl.when(seq >= d)
-        def _():
-            for i in range(2):
-                kv_copy(d, i, (seq, ten)).wait_recv()
-
-    blocks = [slice(e * TOK, (e + 1) * TOK) for e in range(SPAN + 1)]
-    for rows in blocks:
-        kt_s[:, rows] = jnp.transpose(kv_s[0, rows, :].astype(F32)).astype(BF)
-        vt_s[:, rows] = jnp.transpose(kv_s[1, rows, :].astype(F32)).astype(BF)
 
     def pass_on(z):
         for d in range(1, NY):
             y_copy(d, z, lax.rem(y + NY - d, NY)).wait_recv()
         d_copy(z, core).start()
 
-    def attend(head, carry):
-        lanes = pl.ds(aligned(head, TOK), TOK)
-        q = q_s[lanes, :]
-        top = jnp.full((1, TOK), NEG_FILL, F32)
-        for rows in blocks:
-            scores = (
-                lax.dot_general(kv_s[0, rows, :], q, LAST, preferred_element_type=F32) * SCALE
-                + bias_s[rows, :]
-            )
-            s_s[rows, :] = scores
-            top = jnp.maximum(top, jnp.max(scores, axis=0, keepdims=True))
-        total = jnp.zeros((1, TOK), F32)
-        for rows in blocks:
-            raised = jnp.exp(s_s[rows, :] - top)
-            s_s[rows, :] = raised
-            total = total + jnp.sum(raised, axis=0, keepdims=True)
-        inverse = 1.0 / total
-        context = jnp.zeros((DH, TOK), F32)
-        for rows in blocks:
-            weights = (s_s[rows, :] * inverse).astype(BF)
-            p_s[rows, lanes] = weights
-            context = context + jnp.dot(vt_s[:, rows], weights, preferred_element_type=F32)
-        ctx_s[:, pl.ds(aligned(head, DH), DH)] = jnp.transpose(context).astype(BF)
-        for k in (2 * head, 2 * head + 1):
-
-            @pl.when(zl - k >= 0)
-            def _():
-                pass_on(zl - k)
-
-            @pl.when((k > 0) & (zl + k < NZ))
-            def _():
-                pass_on(zl + k)
+    def pass_both(k, carry):
+        @pl.when(zl - k >= 0)
+        def _():
+            pass_on(zl - k)
+
+        @pl.when((k > 0) & (zl + k < NZ))
+        def _():
+            pass_on(zl + k)
 
         return carry
 
-    lax.fori_loop(0, HEADS, attend, 0)
-    for z in range(NZ):
-        d_copy(z, 1 - core).wait_recv()
+    lax.fori_loop(0, NZ // 2, pass_both, 0)
+    lax.fori_loop(0, EARLY - 1, og_forward, 0)
+    lax.fori_loop(NZ // 2, NZ, pass_both, 0)
+
+    def whole():
+        for z in range(NZ):
+            d_copy(z, 1 - core).wait_recv()
+
+    @pl.when(core != away)
+    def _():
+        whole()
 
     def rs_copy(side, place, d):
         return remote(
@@ -305,20 +365,15 @@
         lanes = pl.ds(aligned(xx * SPLIT + j, CHUNK), CHUNK)
         return jnp.dot(ctx_s[...], w_s[half, :, lanes], preferred_element_type=F32).astype(BF)
 
-    def project(side, half):
-        def step(place, carry):
-            d, j = lax.rem(place, NX - 1) + 1, lax.div(place, NX - 1)
-            rs_out[side, place] = share(half, lax.rem(x + d, NX), j)
-            rs_copy(side, place, d).start()
-            return carry
-
-        lax.fori_loop(0, SPLIT * (NX - 1), step, 0)
-
-        def own(j, carry):
+    def project(side, half, send):
+        for j in range(SPLIT):
+            for d in range(1, NX):
+                place = j * (NX - 1) + d - 1
+                rs_out[side, place] = share(half, lax.rem(x + d, NX), j)
+                if send:
+                    rs_copy(side, place, d).start()
+        for j in range(SPLIT):
             rs_own[side, j] = share(half, x, j)
-            return carry
-
-        lax.fori_loop(0, SPLIT, own, 0)
 
     def collect(side, j):
         total = rs_own[side, j].astype(F32)
@@ -328,42 +383,45 @@
             total = total + rs_in[side, place].astype(F32)
         return total
 
-    project(0, away)
-
     def rz_copy(j):
         return remote(zsum_s.at[j], zin_s.at[j], rz_ss.at[j], rz_rs.at[j], partner)
 
-    def og_forward(i):
-        oz_copy(i, away * NX + x).wait_recv()
-        for d in range(1, NX):
-            of_copy(i, d, away * NX + x).start()
-
-    project(1, zh)
-    og_forward(0)
-    for j in range(SPLIT):
+    def grad_part(half):
+        total = jnp.zeros((TOK, WIDTH), F32)
+        for xx in range(NX):
+            total = total + lax.dot_general(
+                g_s[half * NX + xx], w_s[half, :, xx * WIDTH : (xx + 1) * WIDTH], LAST,
+                preferred_element_type=F32,
+            )
+        return total
+
+    project(0, away, True)
+
+    @pl.when(core == away)
+    def _():
+        whole()
+
+    project(1, zh, False)
+    zsum_s[0] = collect(0, 0).astype(BF)
+    rz_copy(0).start()
+    for d in range(1, NX):
+        ox_copy(d, zh * NX + lax.rem(x + NX - d, NX)).wait_recv()
+    acc_s[...] = grad_part(zh)
+    lax.fori_loop(EARLY - 1, PARTS - 2, og_forward, 0)
+    for j in range(1, SPLIT):
         zsum_s[j] = collect(0, j).astype(BF)
         rz_copy(j).start()
-    for i in range(1, ROWS):
-        og_forward(i)
-
-    def grad_part(half):
-        def step(xx, carry):
-            lanes = pl.ds(aligned(xx, WIDTH), WIDTH)
-            acc_s[...] += lax.dot_general(
-                g_s[half * NX + xx], w_s[half, :, lanes], LAST, preferred_element_type=F32
-            )
-            return carry
-
-        lax.fori_loop(0, NX, step, 0)
-
-    acc_s[...] = jnp.zeros_like(acc_s)
-    for d in range(1, NX):
-        ox_copy(d, zh * NX + lax.rem(x + NX - d, NX)).wait_recv()
-    grad_part(zh)
-    for i in range(ROWS):
+    lax.fori_loop(PARTS - 2, PARTS, og_forward, 0)
+    for place in range(SPLIT * (NX - 1)):
+        rs_copy(1, place, place % (NX - 1) + 1).start()
+
+    def og_arrived(i, carry):
         for d in range(1, NX):
             of_copy(i, d, away * NX + lax.rem(x + NX - d, NX)).wait_recv()
-    grad_part(away)
+        return carry
+
+    lax.fori_loop(0, PARTS, og_arrived, 0)
+    acc_s[...] += grad_part(away)
 
     for i in range(HEADS):
         grad = acc_s[:, i * DH : (i + 1) * DH].astype(BF)
@@ -374,20 +432,14 @@
     def gr_copy(d, to):
         return remote(dkv_out.at[d - 1], dkv_in.at[d - 1], gr_ss.at[d - 1], gr_rs.at[d - 1], to)
 
-    dq_s[...] = jnp.zeros_like(dq_s)
     for e, rows in enumerate(blocks):
         d = SPAN - e
         values = kv_s[1, rows, :]
-
-        def back(head, carry):
-            lanes = pl.ds(aligned(head, TOK), TOK)
+        for head in range(HEADS):
+            lanes = slice(head * TOK, (head + 1) * TOK)
             slope = lax.dot_general(values, gh_s[lanes, :], LAST, preferred_element_type=F32)
-            ds_s[:, lanes] = (p_s[rows, lanes].astype(F32) * (slope - delta_s[:, lanes])).astype(BF)
-            dq_s[:, lanes] += jnp.dot(kt_s[:, rows], ds_s[:, lanes], preferred_element_type=F32)
-            return carry
-
-        lax.fori_loop(0, HEADS, back, 0)
-        dk = jnp.dot(ds_s[...], q_s[...], preferred_element_type=F32)
+            ds_s[rows, lanes] = (p_s[rows, lanes].astype(F32) * (slope - delta_s[:, lanes])).astype(BF)
+        dk = jnp.dot(ds_s[rows, :], q_s[...], preferred_element_type=F32)
         dv = jnp.dot(p_s[rows, :], gh_s[...], preferred_element_type=F32)
         if d == 0:
             dkv_own[0] = dk
@@ -401,9 +453,9 @@
                 gr_copy(d, (seq - d, ten)).start()
 
     for i in range(HEADS):
-        gq_s[:, i * DH : (i + 1) * DH] = (
-            jnp.transpose(dq_s[:, i * TOK : (i + 1) * TOK]) * SCALE
-        ).astype(BF)
+        lanes = slice(i * TOK, (i + 1) * TOK)
+        dq = jnp.dot(kt_s[...], ds_s[:, lanes], preferred_element_type=F32)
+        gq_s[:, i * DH : (i + 1) * DH] = (jnp.transpose(dq) * SCALE).astype(BF)
     stores = [pltpu.make_async_copy(gq_s, gq_hbm, store_sem.at[0])]
     stores[0].start()
 
@@ -432,12 +484,17 @@
         stores[-1].start()
 
     sib_copy.wait_send()
+    for n in range(1, SPAN // 2 + 1):
+
+        @pl.when(seq + 2 * n < seqs)
+        def _():
+            kv_copy(n, (seq, ten)).wait_send()
+
+        @pl.when(ks_sent(n))
+        def _():
+            ks_copy(n).wait_send()
+
     for d in range(1, SPAN + 1):
-
-        @pl.when(seq + d < seqs)
-        def _():
-            for i in range(2):
-                kv_copy(d, i, (seq, ten)).wait_send()
 
         @pl.when(seq >= d)
         def _():
@@ -445,10 +502,14 @@
 
     for d in range(1, NX):
         ox_copy(d, ten).wait_send()
-        for i in range(ROWS):
+
+    def sent(i, carry):
+        oz_copy(i, ten).wait_send()
+        for d in range(1, NX):
             of_copy(i, d, away * NX + x).wait_send()
-    for i in range(ROWS):
-        oz_copy(i, ten).wait_send()
+        return carry
+
+    lax.fori_loop(0, PARTS, sent, 0)
 
     def drain(z, carry):
         for d in range(1, NY):
@@ -476,24 +537,24 @@
 
 
 def local(queries, key_rows, value_rows, out_weight, out_grad, doc_lengths):
-    anywhere = pl.BlockSpec(memory_space=pl.ANY)
+    anywhere = pl.BlockSpec(memory_space=pltpu.HBM)
     vmem = pl.BlockSpec(memory_space=pltpu.VMEM)
     dma = pltpu.SemaphoreType.DMA
     places = SPLIT * (NX - 1)
     scratch = [
         ((HEADS * TOK, DH), BF), ((2, KEYS, DH), BF), ((DH, KEYS), BF), ((DH, KEYS), BF),
-        ((KEYS, TOK), F32), ((KEYS, TOK), F32), ((KEYS, HEADS * TOK), BF),
-        ((TOK, WIDTH), BF), ((8, 128), F32),
+        ((KEYS, TOK), F32), ((2, KEYS, TOK), F32), ((KEYS, HEADS * TOK), BF),
+        ((TOK, WIDTH), BF),
         ((2, WIDTH, HALF), BF), ((16, HALF // 2), BF), ((16, HALF // 2), BF),
         ((2 * NX, TOK, WIDTH), BF), ((TOK, WIDTH), F32), ((HEADS * TOK, DH), BF),
-        ((TOK, HEADS * TOK), BF), ((DH, HEADS * TOK), F32), ((1, HEADS * TOK), F32),
+        ((KEYS, HEADS * TOK), BF), ((1, HEADS * TOK), F32),
         ((2, places, TOK, CHUNK), BF), ((2, places, TOK, CHUNK), BF), ((2, SPLIT, TOK, CHUNK), BF),
         ((SPLIT, TOK, CHUNK), BF), ((SPLIT, TOK, CHUNK), BF), ((TOK, WIDTH), BF), ((TOK, WIDTH), BF),
         ((SPAN, 2, TOK, DH), BF), ((SPAN, 2, TOK, DH), BF), ((2, TOK, DH), F32), ((2, TOK, DH), BF),
     ]
     semaphores = [
-        (3 + HEADS,), (4,), (2,), (SPAN, 2), (SPAN, 2), (2, NZ), (2, NZ), (NY - 1, NZ), (NY - 1, NZ),
-        (NZ,), (NZ,), (NX - 1,), (NX - 1,), (ROWS,), (ROWS,), (ROWS, NX - 1), (ROWS, NX - 1),
+        (3 + HEADS,), (4,), (2,), (SPAN // 2,), (SPAN // 2,), (SPAN // 2,), (SPAN // 2,), (2, NZ), (2, NZ), (NY - 1, NZ), (NY - 1, NZ),
+        (NZ,), (NZ,), (NX - 1,), (NX - 1,), (PARTS,), (PARTS,), (PARTS, NX - 1), (PARTS, NX - 1),
         (2, places), (2, places), (SPLIT,), (SPLIT,), (SPAN,), (SPAN,),
     ]
     return pl.pallas_call(
@@ -510,7 +571,7 @@
         scratch_shapes=[pltpu.VMEM(shape, kind) for shape, kind in scratch]
         + [dma(shape) for shape in semaphores],
         compiler_params=pltpu.CompilerParams(
-            collective_id=0, has_side_effects=True, vmem_limit_bytes=48 * 2**20
+            collective_id=0, has_side_effects=True, vmem_limit_bytes=60 * 2**20
         ),
         cost_estimate=pl.CostEstimate(
             flops=5 * 10**9, bytes_accessed=2 * 10**6, transcendentals=1400000

time: 136 us -> 106 us (0.78)
  the two profiles are of different devices: /device:TPU:9 before, /device:TPU:219 now
where the time goes in v2:
time: 106 us
  Pallas kernels  101 us (95%)
  local copies, waits for them, and re-layouts  4.07 us (4%)
    pallas_call x1, Pallas kernels, local(): pl.pallas_call(kernel, name='attention_block', out_shape=[jax.ShapeDtypeS...  101 us
    unnamed x10, local copies, waits for them, and re-layouts  4.07 us

profile of v2, /device:TPU:219, one launch (start us, length us, event | category | flops | bytes accessed | tf_op | source)
XLA Modules:
  0.0 106.1 jit_solution(8538630566510268445)
XLA Ops:
  0.6 101.3 %attention_block.1 = (bf16[256,512]{1,0:T(8,128)(2,1)}, bf16[256,512]{1,0:T(8,128)(2,1)}, bf16[256,128]{1,0:T(8,128)(2,1)}, bf16[256,128]{1,0:T(8,128)(2,1)}) custom-call(bf16[256,512]{1,0:T(8,128)(2,1)} %q_hbm.1, bf16[256,128]{1,0:T(8,128)(2,1)} %k_hbm.1, bf16[256,128]{1,0:T(8,128)(2,1)} %v_hbm.1, bf16[8,4096]{1,0:T(8,128)(2,1)} %w_ref.1, ...), custom_call_target="tpu_custom_call" | custom-call | flops 5000000000 | bytes 2000000 | tf_op jit(solution)/shard_map/attention_block/pallas_call | solution.py:560
  102.0 0.0 copy-start
  102.0 1.7 %copy.14 = bf16[256,512]{1,0:T(8,128)(2,1)} copy(bf16[256,512]{1,0:T(8,128)(2,1)} %get-tuple-element.8) | data formatting | bytes 524288
  103.7 0.0 copy-done
  103.7 0.0 copy-start.2
  103.7 0.7 copy.15
  104.4 0.2 copy-done.2
  104.6 0.0 copy-start.1
  104.6 0.6 copy.16
  105.2 0.2 copy-done.1
  105.4 0.6 copy.17
Async XLA Ops:
  102.0 1.7 %copy-start = (bf16[256,512]{1,0:T(8,128)(2,1)S(1)}, bf16[256,512]{1,0:T(8,128)(2,1)}, u32[]{:S(2)}) copy-start(bf16[256,512]{1,0:T(8,128)(2,1)} %get-tuple-element.9) | copy-start | bytes 786436
  103.7 0.9 copy-start.2
  104.6 0.9 copy-start.1

commit v3 on v2

--- a/solution.py
+++ b/solution.py
@@ -15,6 +15,7 @@
 WIDTH = HEADS * DH
 KEYS = (SPAN + 1) * TOK
 HALF = NX * WIDTH
+SIDE = HALF // 2
 CHUNK = 256
 SPLIT = WIDTH // CHUNK
 PARTS = 8
@@ -44,9 +45,9 @@
     q_s, kv_s, vt_s, kt_s, bias_s, s_s, p_s, ctx_s,
     w_s, wout_s, win_s, g_s, acc_s, gh_s, ds_s, delta_s,
     rs_out, rs_in, rs_own, zsum_s, zin_s, attn_s, gq_s,
-    dkv_out, dkv_in, dkv_own, gkv_s,
-    load_sem, store_sem, sib_sem, kv_ss, kv_rs, ks_ss, ks_rs, z_ss, z_rs, y_ss, y_rs, d_ss, d_rs,
-    ox_ss, ox_rs, oz_ss, oz_rs, of_ss, of_rs, rs_ss, rs_rs, rz_ss, rz_rs, gr_ss, gr_rs,
+    dkv_out, dkv_in, dkv_own, gkv_s, odd_out, odd_in, dkv_f,
+    load_sem, store_sem, sib_sem, kv_ss, kv_rs, ks_ss, ks_rs, z_ss, z_rs, y_ss, y_rs, d_ss, d_rs, yl_ss, yl_rs, dl_ss, dl_rs,
+    ox_ss, ox_rs, oz_ss, oz_rs, of_ss, of_rs, rs_ss, rs_rs, rz_ss, rz_rs, gr_ss, gr_rs, go_ss, go_rs,
 ):
     seq = lax.axis_index("seq")
     ten = lax.axis_index("tensor")
@@ -106,29 +107,33 @@
 
     expected = expected + up_ok.astype(jnp.int32) + down_ok.astype(jnp.int32)
     for d in range(1, SPAN + 1):
-        ahead, behind = seq + d < seqs, seq >= d
+        @pl.when(seq < d)
+        def _():
+            kv_s[:, (SPAN - d) * TOK : (SPAN - d + 1) * TOK, :] = jnp.zeros((2, TOK, DH), BF)
+
+    for n in range(1, SPAN // 2 + 1):
+        ahead, behind = seq + 2 * n < seqs, seq >= 2 * n
 
         @pl.when(ahead)
         def _():
-            greet((seq + d, ten))
+            greet((seq + 2 * n, ten))
 
         @pl.when(behind)
         def _():
-            greet((seq - d, ten))
+            greet((seq - 2 * n, ten))
 
         @pl.when(jnp.logical_not(ahead))
         def _():
-            dkv_in[d - 1] = jnp.zeros((2, TOK, DH), BF)
-
-        @pl.when(jnp.logical_not(behind))
-        def _():
-            kv_s[:, (SPAN - d) * TOK : (SPAN - d + 1) * TOK, :] = jnp.zeros((2, TOK, DH), BF)
+            dkv_in[n - 1] = jnp.zeros((2, TOK, DH), BF)
 
         expected = expected + ahead.astype(jnp.int32) + behind.astype(jnp.int32)
 
-    mine = w_ref[:, pl.ds(aligned(core, HALF), HALF)].astype(F32)
-    other = w_ref[:, pl.ds(aligned(1 - core, HALF), HALF)].astype(F32)
-    wout_s[...] = jnp.concatenate([other[:, : HALF // 2], other[:, HALF // 2 :]], axis=0).astype(BF)
+    def side_of(half, which):
+        start = pl.multiple_of(half * HALF + which * SIDE, SIDE)
+        return w_ref[:, pl.ds(start, SIDE)].astype(F32)
+
+    mine = [side_of(half, core) for half in range(2)]
+    wout_s[...] = jnp.concatenate([side_of(half, 1 - core) for half in range(2)], axis=0).astype(BF)
 
     lengths = len_ref[...]
     docs = lengths.shape[1]
@@ -184,61 +189,81 @@
     def ks_sent(n):
         return seq >= 2 * n - 2 + 2 * core
 
-    def w_rows(z, yy):
-        return w_s.at[core, pl.ds(aligned(z * NY + yy, 16), 16)]
-
-    def z_copy(way, hop, z):
+    def send_keys():
+        for n in range(1, SPAN // 2 + 1):
+
+            @pl.when(seq + 2 * n < seqs)
+            def _():
+                kv_copy(n, (seq + 2 * n, ten)).start()
+
+    send_keys()
+
+    def z_copy(way, hop, z, part):
         to = (seq + 2 * NY, ten) if way == 0 else (seq - 2 * NY, ten)
-        return remote(w_rows(z, y), w_rows(z, y), z_ss.at[way, hop], z_rs.at[way, hop], to)
+        half = zh if part else away
+        rows = w_s.at[half, z, pl.ds(aligned(y, 16), 16), pl.ds(aligned(core, SIDE), SIDE)]
+        return remote(rows, rows, z_ss.at[way, hop, part], z_rs.at[way, hop, part], to)
 
     def y_copy(d, z, yy):
-        return remote(w_rows(z, yy), w_rows(z, yy), y_ss.at[d - 1, z], y_rs.at[d - 1, z], at_y(d))
-
-    def d_copy(z, half):
-        rows = w_s.at[half, pl.ds(aligned(z, NY * 16), NY * 16)]
+        rows = w_s.at[away, z, pl.ds(aligned(yy, 16), 16), pl.ds(aligned(core, SIDE), SIDE)]
+        return remote(rows, rows, y_ss.at[d - 1, z], y_rs.at[d - 1, z], at_y(d))
+
+    def d_copy(z, which):
+        rows = w_s.at[away, z, :, pl.ds(aligned(which, SIDE), SIDE)]
         return remote(rows, rows, d_ss.at[z], d_rs.at[z], sibling)
 
+    def y_late(d, yy):
+        rows = w_s.at[zh, :, pl.ds(aligned(yy, 16), 16), pl.ds(aligned(core, SIDE), SIDE)]
+        return remote(rows, rows, yl_ss.at[d - 1], yl_rs.at[d - 1], at_y(d))
+
+    def d_late(d, which):
+        yy = lax.rem(y + NY - d, NY)
+        rows = w_s.at[zh, :, pl.ds(aligned(yy, 16), 16), pl.ds(aligned(which, SIDE), SIDE)]
+        return remote(rows, rows, dl_ss.at[d], dl_rs.at[d], sibling)
+
     sib_copy.wait_recv()
-    came = win_s[...].astype(F32)
-    came = jnp.concatenate([came[:8], came[8:]], axis=1)
-    upper = jnp.where(core == 0, mine, came)
-    lower = jnp.where(core == 0, came, mine)
-    w_s[core, pl.ds(aligned(chip, 16), 16), :] = jnp.concatenate([upper, lower], axis=0).astype(BF)
-
-    @pl.when(up_ok)
-    def _():
-        z_copy(0, 0, zl).start()
-
-    @pl.when(down_ok)
-    def _():
-        z_copy(1, 0, zl).start()
+    for half in range(2):
+        came = win_s[...].astype(F32)[half * 8 : half * 8 + 8]
+        upper = jnp.where(core == 0, mine[half], came)
+        lower = jnp.where(core == 0, came, mine[half])
+        w_s[half, zl, pl.ds(aligned(y, 16), 16), pl.ds(aligned(core, SIDE), SIDE)] = jnp.concatenate(
+            [upper, lower], axis=0
+        ).astype(BF)
+
+    for part in range(2):
+
+        @pl.when(up_ok)
+        def _():
+            z_copy(0, 0, zl, part).start()
+
+        @pl.when(down_ok)
+        def _():
+            z_copy(1, 0, zl, part).start()
 
     for d in range(1, NY):
         y_copy(d, zl, y).start()
-    for n in range(1, SPAN // 2 + 1):
-
-        @pl.when(seq + 2 * n < seqs)
-        def _():
-            kv_copy(n, (seq + 2 * n, ten)).start()
-
-    def z_step(hop):
+
+    def z_step(hop, part):
         below, above = zl - hop, zl + hop
 
         @pl.when(below >= 0)
         def _():
-            z_copy(0, hop - 1, below).wait_recv()
+            z_copy(0, hop - 1, below, part).wait_recv()
 
             @pl.when(up_ok)
             def _():
-                z_copy(0, hop, below).start()
+                z_copy(0, hop, below, part).start()
 
         @pl.when(above < NZ)
         def _():
-            z_copy(1, hop - 1, above).wait_recv()
+            z_copy(1, hop - 1, above, part).wait_recv()
 
             @pl.when(down_ok)
             def _():
-                z_copy(1, hop, above).start()
+                z_copy(1, hop, above, part).start()
+
+    def y_step(hop):
+        below, above = zl - hop, zl + hop
 
         @pl.when(below >= 0)
         def _():
@@ -311,19 +336,13 @@
 
     oz_copy(0, ten).start()
     for hop in range(1, NZ):
-        z_step(hop)
+        z_step(hop, 0)
+        y_step(hop)
+        if hop > 1:
+            z_step(hop - 1, 1)
         if hop in (2, 4, 6):
             oz_copy(hop // 2, ten).start()
-        if hop == 3:
-            share_keys()
-        if hop == 4:
-            for copy in loads[2:]:
-                copy.wait()
-            turn_keys()
-        if hop == 5:
-            attend((0, 1))
-        if hop == 6:
-            attend((2, 3))
+    z_step(NZ - 1, 1)
     for i in range(EARLY, PARTS):
         oz_copy(i, ten).start()
 
@@ -343,17 +362,21 @@
 
         return carry
 
+    for copy in loads[2:]:
+        copy.wait()
+    share_keys()
+    lax.fori_loop(0, EARLY - 1, og_forward, 0)
     lax.fori_loop(0, NZ // 2, pass_both, 0)
-    lax.fori_loop(0, EARLY - 1, og_forward, 0)
-    lax.fori_loop(NZ // 2, NZ, pass_both, 0)
-
-    def whole():
-        for z in range(NZ):
-            d_copy(z, 1 - core).wait_recv()
-
-    @pl.when(core != away)
-    def _():
-        whole()
+    turn_keys()
+    attend((0, 1))
+    lax.fori_loop(NZ // 2, NZ - 1, pass_both, 0)
+    attend((2, 3))
+    lax.fori_loop(NZ - 1, NZ, pass_both, 0)
+    for d in range(1, NY):
+        y_late(d, y).start()
+    d_late(0, core).start()
+    for z in range(NZ):
+        d_copy(z, 1 - core).wait_recv()
 
     def rs_copy(side, place, d):
         return remote(
@@ -363,15 +386,15 @@
 
     def share(half, xx, j):
         lanes = pl.ds(aligned(xx * SPLIT + j, CHUNK), CHUNK)
-        return jnp.dot(ctx_s[...], w_s[half, :, lanes], preferred_element_type=F32).astype(BF)
-
-    def project(side, half, send):
+        columns = w_s[half, :, :, lanes].reshape(WIDTH, CHUNK)
+        return jnp.dot(ctx_s[...], columns, preferred_element_type=F32).astype(BF)
+
+    def project(side, half):
         for j in range(SPLIT):
             for d in range(1, NX):
                 place = j * (NX - 1) + d - 1
                 rs_out[side, place] = share(half, lax.rem(x + d, NX), j)
-                if send:
-                    rs_copy(side, place, d).start()
+                rs_copy(side, place, d).start()
         for j in range(SPLIT):
             rs_own[side, j] = share(half, x, j)
 
@@ -390,30 +413,30 @@
         total = jnp.zeros((TOK, WIDTH), F32)
         for xx in range(NX):
             total = total + lax.dot_general(
-                g_s[half * NX + xx], w_s[half, :, xx * WIDTH : (xx + 1) * WIDTH], LAST,
+                g_s[half * NX + xx],
+                w_s[half, :, :, xx * WIDTH : (xx + 1) * WIDTH].reshape(WIDTH, WIDTH),
+                LAST,
                 preferred_element_type=F32,
             )
         return total
 
-    project(0, away, True)
-
-    @pl.when(core == away)
-    def _():
-        whole()
-
-    project(1, zh, False)
+    project(0, away)
     zsum_s[0] = collect(0, 0).astype(BF)
     rz_copy(0).start()
+    og_forward(EARLY - 1)
+    for j in range(1, SPLIT):
+        zsum_s[j] = collect(0, j).astype(BF)
+        rz_copy(j).start()
+    for d in range(1, NY):
+        y_late(d, lax.rem(y + NY - d, NY)).wait_recv()
+        d_late(d, core).start()
+    lax.fori_loop(EARLY, PARTS, og_forward, 0)
+    for d in range(NY):
+        d_late(d, 1 - core).wait_recv()
+    project(1, zh)
     for d in range(1, NX):
         ox_copy(d, zh * NX + lax.rem(x + NX - d, NX)).wait_recv()
     acc_s[...] = grad_part(zh)
-    lax.fori_loop(EARLY - 1, PARTS - 2, og_forward, 0)
-    for j in range(1, SPLIT):
-        zsum_s[j] = collect(0, j).astype(BF)
-        rz_copy(j).start()
-    lax.fori_loop(PARTS - 2, PARTS, og_forward, 0)
-    for place in range(SPLIT * (NX - 1)):
-        rs_copy(1, place, place % (NX - 1) + 1).start()
 
     def og_arrived(i, carry):
         for d in range(1, NX):
@@ -429,28 +452,45 @@
         product = grad.astype(F32) * ctx_s[:, i * DH : (i + 1) * DH].astype(F32)
         delta_s[:, i * TOK : (i + 1) * TOK] = jnp.sum(jnp.transpose(product), axis=0, keepdims=True)
 
-    def gr_copy(d, to):
-        return remote(dkv_out.at[d - 1], dkv_in.at[d - 1], gr_ss.at[d - 1], gr_rs.at[d - 1], to)
-
-    for e, rows in enumerate(blocks):
-        d = SPAN - e
+    def gr_copy(n, to):
+        return remote(dkv_out.at[n - 1], dkv_in.at[n - 1], gr_ss.at[n - 1], gr_rs.at[n - 1], to)
+
+    def odd_copy(n):
+        return remote(odd_out.at[n], odd_in.at[n], go_ss.at[n], go_rs.at[n], sibling)
+
+    def back(d):
+        rows = blocks[SPAN - d]
         values = kv_s[1, rows, :]
         for head in range(HEADS):
             lanes = slice(head * TOK, (head + 1) * TOK)
             slope = lax.dot_general(values, gh_s[lanes, :], LAST, preferred_element_type=F32)
             ds_s[rows, lanes] = (p_s[rows, lanes].astype(F32) * (slope - delta_s[:, lanes])).astype(BF)
-        dk = jnp.dot(ds_s[rows, :], q_s[...], preferred_element_type=F32)
-        dv = jnp.dot(p_s[rows, :], gh_s[...], preferred_element_type=F32)
-        if d == 0:
-            dkv_own[0] = dk
-            dkv_own[1] = dv
-        else:
-            dkv_out[d - 1, 0] = dk.astype(BF)
-            dkv_out[d - 1, 1] = dv.astype(BF)
-
-            @pl.when(seq >= d)
-            def _():
-                gr_copy(d, (seq - d, ten)).start()
+        return (
+            jnp.dot(ds_s[rows, :], q_s[...], preferred_element_type=F32),
+            jnp.dot(p_s[rows, :], gh_s[...], preferred_element_type=F32),
+        )
+
+    for n in range(SPAN // 2 - 1, -1, -1):
+        for i, part in enumerate(back(2 * n + 1)):
+            odd_out[n, i] = part.astype(BF)
+        odd_copy(n).start()
+    for n in range(SPAN // 2, 0, -1):
+        for i, part in enumerate(back(2 * n)):
+            dkv_f[n - 1, i] = part
+    for n in range(SPAN // 2):
+        odd_copy(n).wait_recv()
+    for n in range(SPAN // 2, 0, -1):
+        for i in range(2):
+            from_one = odd_in[n - 1, i].astype(F32)
+            from_two = odd_in[n, i].astype(F32) if n < SPAN // 2 else jnp.zeros((TOK, DH), F32)
+            dkv_out[n - 1, i] = (dkv_f[n - 1, i] + jnp.where(core == 0, from_two, from_one)).astype(BF)
+
+        @pl.when(seq >= 2 * n)
+        def _():
+            gr_copy(n, (seq - 2 * n, ten)).start()
+
+    for i, part in enumerate(back(0)):
+        dkv_own[i] = part + jnp.where(core == 0, odd_in[0, i].astype(F32), 0.0)
 
     for i in range(HEADS):
         lanes = slice(i * TOK, (i + 1) * TOK)
@@ -467,16 +507,16 @@
     stores.append(pltpu.make_async_copy(attn_s, out_hbm, store_sem.at[1]))
     stores[1].start()
 
-    for d in range(1, SPAN + 1):
-
-        @pl.when(seq + d < seqs)
-        def _():
-            gr_copy(d, (seq, ten)).wait_recv()
+    for n in range(1, SPAN // 2 + 1):
+
+        @pl.when(seq + 2 * n < seqs)
+        def _():
+            gr_copy(n, (seq, ten)).wait_recv()
 
     for i in range(2):
         total = dkv_own[i]
-        for d in range(1, SPAN + 1):
-            total = total + dkv_in[d - 1, i].astype(F32)
+        for n in range(1, SPAN // 2 + 1):
+            total = total + dkv_in[n - 1, i].astype(F32)
         gkv_s[i] = ((total * SCALE) if i == 0 else total).astype(BF)
         stores.append(
             pltpu.make_async_copy(gkv_s.at[i], (gk_hbm, gv_hbm)[i], store_sem.at[2 + i])
@@ -494,12 +534,16 @@
         def _():
             ks_copy(n).wait_send()
 
-    for d in range(1, SPAN + 1):
-
-        @pl.when(seq >= d)
-        def _():
-            gr_copy(d, (seq, ten)).wait_send()
-
+        @pl.when(seq >= 2 * n)
+        def _():
+            gr_copy(n, (seq, ten)).wait_send()
+
+        odd_copy(n - 1).wait_send()
+
+    for d in range(1, NY):
+        y_late(d, y).wait_send()
+    for d in range(NY):
+        d_late(d, core).wait_send()
     for d in range(1, NX):
         ox_copy(d, ten).wait_send()
 
@@ -516,13 +560,15 @@
             y_copy(d, z, y).wait_send()
         d_copy(z, core).wait_send()
 
-        @pl.when((z <= zl) & up_ok)
-        def _():
-            z_copy(0, z, zl).wait_send()
-
-        @pl.when((z < NZ - zl) & down_ok)
-        def _():
-            z_copy(1, z, zl).wait_send()
+        for part in range(2):
+
+            @pl.when((z <= zl) & up_ok)
+            def _():
+                z_copy(0, z, zl, part).wait_send()
+
+            @pl.when((z < NZ - zl) & down_ok)
+            def _():
+                z_copy(1, z, zl, part).wait_send()
 
         return carry
 
@@ -534,6 +580,11 @@
         rz_copy(j).wait_send()
     for copy in stores:
         copy.wait()
+
+
+def write(*refs):
+    for i in range(4):
+        refs[4 + i][...] = refs[i][...]
 
 
 def local(queries, key_rows, value_rows, out_weight, out_grad, doc_lengths):
@@ -545,19 +596,20 @@
         ((HEADS * TOK, DH), BF), ((2, KEYS, DH), BF), ((DH, KEYS), BF), ((DH, KEYS), BF),
         ((KEYS, TOK), F32), ((2, KEYS, TOK), F32), ((KEYS, HEADS * TOK), BF),
         ((TOK, WIDTH), BF),
-        ((2, WIDTH, HALF), BF), ((16, HALF // 2), BF), ((16, HALF // 2), BF),
+        ((2, NZ, NY * 16, HALF), BF), ((16, SIDE), BF), ((16, SIDE), BF),
         ((2 * NX, TOK, WIDTH), BF), ((TOK, WIDTH), F32), ((HEADS * TOK, DH), BF),
         ((KEYS, HEADS * TOK), BF), ((1, HEADS * TOK), F32),
         ((2, places, TOK, CHUNK), BF), ((2, places, TOK, CHUNK), BF), ((2, SPLIT, TOK, CHUNK), BF),
         ((SPLIT, TOK, CHUNK), BF), ((SPLIT, TOK, CHUNK), BF), ((TOK, WIDTH), BF), ((TOK, WIDTH), BF),
-        ((SPAN, 2, TOK, DH), BF), ((SPAN, 2, TOK, DH), BF), ((2, TOK, DH), F32), ((2, TOK, DH), BF),
+        ((SPAN // 2, 2, TOK, DH), BF), ((SPAN // 2, 2, TOK, DH), BF), ((2, TOK, DH), F32), ((2, TOK, DH), BF),
+        ((SPAN // 2, 2, TOK, DH), BF), ((SPAN // 2, 2, TOK, DH), BF), ((SPAN // 2, 2, TOK, DH), F32),
     ]
     semaphores = [
-        (3 + HEADS,), (4,), (2,), (SPAN // 2,), (SPAN // 2,), (SPAN // 2,), (SPAN // 2,), (2, NZ), (2, NZ), (NY - 1, NZ), (NY - 1, NZ),
-        (NZ,), (NZ,), (NX - 1,), (NX - 1,), (PARTS,), (PARTS,), (PARTS, NX - 1), (PARTS, NX - 1),
-        (2, places), (2, places), (SPLIT,), (SPLIT,), (SPAN,), (SPAN,),
+        (3 + HEADS,), (4,), (2,), (SPAN // 2,), (SPAN // 2,), (SPAN // 2,), (SPAN // 2,), (2, NZ, 2), (2, NZ, 2), (NY - 1, NZ), (NY - 1, NZ),
+        (NZ,), (NZ,), (NY - 1,), (NY - 1,), (NY,), (NY,), (NX - 1,), (NX - 1,), (PARTS,), (PARTS,), (PARTS, NX - 1), (PARTS, NX - 1),
+        (2, places), (2, places), (SPLIT,), (SPLIT,), (SPAN // 2,), (SPAN // 2,), (SPAN // 2,), (SPAN // 2,),
     ]
-    return pl.pallas_call(
+    results = pl.pallas_call(
         kernel,
         name="attention_block",
         out_shape=[
@@ -577,6 +629,14 @@
             flops=5 * 10**9, bytes_accessed=2 * 10**6, transcendentals=1400000
         ),
     )(queries, key_rows, value_rows, out_weight, out_grad, doc_lengths.reshape(1, -1))
+    return pl.pallas_call(
+        write,
+        name="write_results",
+        out_shape=[jax.ShapeDtypeStruct(each.shape, BF) for each in results],
+        in_specs=[vmem] * 4,
+        out_specs=[vmem] * 4,
+        compiler_params=pltpu.CompilerParams(vmem_limit_bytes=60 * 2**20),
+    )(*results)
 
 
 def solution(mesh):

time: 106 us -> 104 us (0.981)
  the two profiles are of different devices: /device:TPU:219 before, /device:TPU:216 now
where the time goes in v3:
time: 104 us; the launch traced here: 103 us
  Pallas kernels  103 us (99%)
    pallas_call x1, Pallas kernels, local(): pl.pallas_call(kernel, name='attention_block', out_shape=[jax.ShapeDtypeS...  101 us

profile of v3, /device:TPU:216, one launch (start us, length us, event | category | flops | bytes accessed | tf_op | source)
XLA Modules:
  0.0 103.3 jit_solution(1230153509865536721)
XLA Ops:
  0.6 100.8 %attention_block.1 = (bf16[256,512]{1,0:T(8,128)(2,1)}, bf16[256,512]{1,0:T(8,128)(2,1)}, bf16[256,128]{1,0:T(8,128)(2,1)}, bf16[256,128]{1,0:T(8,128)(2,1)}) custom-call(bf16[256,512]{1,0:T(8,128)(2,1)} %q_hbm.1, bf16[256,128]{1,0:T(8,128)(2,1)} %k_hbm.1, bf16[256,128]{1,0:T(8,128)(2,1)} %v_hbm.1, bf16[8,4096]{1,0:T(8,128)(2,1)} %w_ref.1, ...), custom_call_target="tpu_custom_call" | custom-call | flops 5000000000 | bytes 2000000 | tf_op jit(solution)/shard_map/attention_block/pallas_call | solution.py:612
  101.5 1.9 %write_results.1 = (bf16[256,512]{1,0:T(8,128)(2,1)}, bf16[256,512]{1,0:T(8,128)(2,1)}, bf16[256,128]{1,0:T(8,128)(2,1)}, bf16[256,128]{1,0:T(8,128)(2,1)}) custom-call(bf16[256,512]{1,0:T(8,128)(2,1)} %get-tuple-element.8.refs_0_, bf16[256,512]{1,0:T(8,128)(2,1)} %get-tuple-element.9.refs_1_, bf16[256,128]{1,0:T(8,128)(2,1)} %get-tuple-element.10.refs_2_, ...), custom_call_target="tpu_custom_call" | custom-call | tf_op jit(solution)/shard_map/write_results/pallas_call | solution.py:632

commit v4 on v3

--- a/solution.py
+++ b/solution.py
@@ -340,8 +340,8 @@
         y_step(hop)
         if hop > 1:
             z_step(hop - 1, 1)
-        if hop in (2, 4, 6):
-            oz_copy(hop // 2, ten).start()
+        if hop in (2, 3, 4):
+            oz_copy(hop - 1, ten).start()
     z_step(NZ - 1, 1)
     for i in range(EARLY, PARTS):
         oz_copy(i, ten).start()
@@ -427,10 +427,10 @@
     for j in range(1, SPLIT):
         zsum_s[j] = collect(0, j).astype(BF)
         rz_copy(j).start()
+    lax.fori_loop(EARLY, PARTS, og_forward, 0)
     for d in range(1, NY):
         y_late(d, lax.rem(y + NY - d, NY)).wait_recv()
         d_late(d, core).start()
-    lax.fori_loop(EARLY, PARTS, og_forward, 0)
     for d in range(NY):
         d_late(d, 1 - core).wait_recv()
     project(1, zh)

time: 104 us -> 99.1 us (0.953)
  the two profiles are of different devices: /device:TPU:216 before, /device:TPU:9 now
where the time goes in v4:
time: 99.1 us; the launch traced here: 98.8 us
  Pallas kernels  98.2 us (99%)
    pallas_call x1, Pallas kernels, local(): pl.pallas_call(kernel, name='attention_block', out_shape=[jax.ShapeDtypeS...  96.3 us

profile of v4, /device:TPU:9, one launch (start us, length us, event | category | flops | bytes accessed | tf_op | source)
XLA Modules:
  0.0 98.8 jit_solution(1535688889667390957)
XLA Ops:
  0.6 96.3 %attention_block.1 = (bf16[256,512]{1,0:T(8,128)(2,1)}, bf16[256,512]{1,0:T(8,128)(2,1)}, bf16[256,128]{1,0:T(8,128)(2,1)}, bf16[256,128]{1,0:T(8,128)(2,1)}) custom-call(bf16[256,512]{1,0:T(8,128)(2,1)} %q_hbm.1, bf16[256,128]{1,0:T(8,128)(2,1)} %k_hbm.1, bf16[256,128]{1,0:T(8,128)(2,1)} %v_hbm.1, bf16[8,4096]{1,0:T(8,128)(2,1)} %w_ref.1, ...), custom_call_target="tpu_custom_call" | custom-call | flops 5000000000 | bytes 2000000 | tf_op jit(solution)/shard_map/attention_block/pallas_call | solution.py:612
  97.0 1.9 %write_results.1 = (bf16[256,512]{1,0:T(8,128)(2,1)}, bf16[256,512]{1,0:T(8,128)(2,1)}, bf16[256,128]{1,0:T(8,128)(2,1)}, bf16[256,128]{1,0:T(8,128)(2,1)}) custom-call(bf16[256,512]{1,0:T(8,128)(2,1)} %get-tuple-element.8.refs_0_, bf16[256,512]{1,0:T(8,128)(2,1)} %get-tuple-element.9.refs_1_, bf16[256,128]{1,0:T(8,128)(2,1)} %get-tuple-element.10.refs_2_, ...), custom_call_target="tpu_custom_call" | custom-call | tf_op jit(solution)/shard_map/write_results/pallas_call | solution.py:632
